TPU v7x, 1024 devices: a whole 4x4x32 slice. The times are simulated.
1024 devices in a mesh: section: 16 (over x, z_hi), dp: 8 (over y, core), head: 8 (over z_lo).
Axes of the slice: x: 4, y: 4, z: 32 (z_hi: 4, z_lo: 8; z = z_hi * 8 + z_lo), core: 2. Of those that a mesh axis runs over, the one named last changes fastest.
Arguments:
- queries: bfloat16 [2, 16, 1024, 12288], P(None, 'section', 'dp', 'head'), may hold values from -40 to 40
- latents: bfloat16 [2, 16, 1024, 576], P(None, 'section', 'dp'), may hold values from -6 to 6
- out_grad: bfloat16 [2, 16, 1024, 8192], P(None, 'section', 'dp', 'head'), may hold values from -6 to 6
- segment_ids: int32 [2, 16, 1024], P(None, 'section', 'dp'), may hold values from 0 to 31, never falling along the last dimension, each value on 1 to 128 neighbouring positions
- up_weight: bfloat16 [2, 16, 512, 16384], P(None, 'section', None, 'head'), may hold values from -0.25 to 0.25
Outputs:
- query_grad: bfloat16 [2, 16, 1024, 12288], P(None, 'section', 'dp', 'head')
- latent_grad: bfloat16 [2, 16, 1024, 576], P(None, 'section', ('dp', 'head'))
- weight_grad: float32 [16, 512, 16384], P('section', 'dp', 'head')
All inputs are finite; a program needn't handle non-finite values.
Results may differ from a plain program's by a relative error of at most 0.017.
Values may be sent and summed in bfloat16 or wider, within the bound.
No kernel may reach another device: no remote copies, remote signals or barrier semaphores. Data moves between devices by JAX's collectives and lax.ppermute only.
A program may use at most 64 MiB of HBM per device.

v0:
```python
import jax
import jax.numpy as jnp
from jax import lax
from jax.sharding import PartitionSpec as P

LATENT = 512
ROPE = 64
NOPE = 128
VDIM = 128


def in_blocks(x, dim, peers):
    shape = x.shape
    blocks = x.reshape(*shape[:dim], peers, shape[dim] // peers, *shape[dim + 1 :])
    return jnp.moveaxis(blocks, dim, 0)


def summed_on_arrival(x, axis, dim):
    blocks = in_blocks(x, dim, lax.axis_size(axis))
    arrived = lax.all_to_all(blocks, axis, split_axis=0, concat_axis=0, tiled=True)
    return arrived.astype(jnp.float32).sum(axis=0)


def from_behind(block, axis, distance):
    devices = range(lax.axis_size(axis))
    route = [(i - distance, i) for i in devices if i - distance in devices]
    return lax.ppermute(block, axis, route)


def head_grads(queries, latents, out_grad, segment_ids, weight):
    tokens = queries.shape[0]
    heads_here = weight.shape[1] // (NOPE + VDIM)
    latent_plain = latents[:, :LATENT]
    key_rope = latents[:, LATENT:]
    kv_full = jnp.dot(latent_plain, weight, preferred_element_type=jnp.float32).astype(jnp.bfloat16)
    kv_full = kv_full.reshape(tokens, heads_here, NOPE + VDIM)
    key_plain = kv_full[..., :NOPE]
    values = kv_full[..., NOPE:]
    query_heads = queries.reshape(tokens, heads_here, NOPE + ROPE)
    query_plain = query_heads[..., :NOPE]
    query_rope = query_heads[..., NOPE:]
    out_heads = out_grad.reshape(tokens, heads_here, VDIM)
    scale = (NOPE + ROPE) ** (-0.5)
    positions = jnp.arange(tokens)
    allowed = (positions[:, None] >= positions[None, :]) & (
        segment_ids[:, None] == segment_ids[None, :]
    )
    scores = jnp.einsum("thd,shd->hts", query_plain, key_plain, preferred_element_type=jnp.float32)
    scores = scores + jnp.einsum(
        "thd,sd->hts", query_rope, key_rope, preferred_element_type=jnp.float32
    )
    scores = jnp.where(allowed[None], scores * scale, jnp.float32(-1e30))
    top = jnp.max(scores, axis=-1, keepdims=True)
    powers = jnp.exp(scores - top)
    probs = powers / jnp.sum(powers, axis=-1, keepdims=True)
    grad_probs = jnp.einsum("thd,shd->hts", out_heads, values, preferred_element_type=jnp.float32)
    delta = jnp.sum(probs * grad_probs, axis=-1, keepdims=True)
    score_grad = (probs * (grad_probs - delta) * scale).astype(jnp.bfloat16)
    probs_low = probs.astype(jnp.bfloat16)
    value_grad = jnp.einsum(
        "hts,thd->shd", probs_low, out_heads, preferred_element_type=jnp.float32
    )
    key_grad = jnp.einsum(
        "hts,thd->shd", score_grad, query_plain, preferred_element_type=jnp.float32
    )
    rope_grad = jnp.einsum(
        "hts,thd->sd", score_grad, query_rope, preferred_element_type=jnp.float32
    )
    grad_plain = jnp.einsum(
        "hts,shd->thd", score_grad, key_plain, preferred_element_type=jnp.float32
    )
    grad_rope = jnp.einsum("hts,sd->thd", score_grad, key_rope, preferred_element_type=jnp.float32)
    query_grad = (
        jnp.concatenate([grad_plain, grad_rope], -1).reshape(tokens, -1).astype(jnp.bfloat16)
    )
    kv_grad = jnp.concatenate([key_grad, value_grad], -1).reshape(tokens, -1).astype(jnp.bfloat16)
    return (query_grad, kv_grad, rope_grad, latent_plain)


def latent_sum(kv_grad, rope_grad, weight):
    latent_rows = lax.dot_general(
        kv_grad, weight, (((1,), (1,)), ((), ())), preferred_element_type=jnp.float32
    )
    return summed_on_arrival(
        jnp.concatenate([latent_rows, rope_grad], 1).astype(jnp.bfloat16), "head", 0
    ).astype(jnp.bfloat16)


def weight_rows(latent_plain, kv_grad):
    return lax.dot_general(
        latent_plain, kv_grad, (((0,), (0,)), ((), ())), preferred_element_type=jnp.float32
    )


def body(queries, latents, out_grad, segment_ids, up_weight):
    results = []
    for side in range(2):
        results.append(
            head_grads(
                queries[side, 0],
                latents[side, 0],
                out_grad[side, 0],
                segment_ids[side, 0],
                up_weight[side, 0],
            )
        )
    latent_parts = []
    for side in range(2):
        latent_parts.append(latent_sum(results[side][1], results[side][2], up_weight[side, 0]))
    width = up_weight.shape[3]
    forward_term = weight_rows(results[0][3], results[0][1])
    reverse_term = weight_rows(results[1][3], results[1][1])
    forward_part, mirrored = (
        lax.psum_scatter(
            forward_term.astype(jnp.bfloat16), "dp", scatter_dimension=0, tiled=True
        ).astype(jnp.float32),
        lax.psum_scatter(
            reverse_term.astype(jnp.bfloat16), "dp", scatter_dimension=0, tiled=True
        ).astype(jnp.float32),
    )
    section_count = lax.axis_size("section")
    shard_rows = mirrored.shape[0]
    pieces = mirrored.reshape(shard_rows, section_count, width // section_count)
    spread = lax.all_to_all(
        pieces.astype(jnp.bfloat16), "section", split_axis=1, concat_axis=1, tiled=True
    ).astype(pieces.dtype)
    flipped = spread[:, ::-1, :]
    gathered = lax.all_to_all(
        flipped.astype(jnp.bfloat16), "section", split_axis=1, concat_axis=1, tiled=True
    ).astype(flipped.dtype)
    mirrored = gathered.reshape(shard_rows, width)
    weight_grad = (forward_part + mirrored)[None]
    query_fwd, latent_fwd = from_behind((results[0][0], latent_parts[0]), "section", -1)
    query_rev, latent_rev = from_behind((results[1][0], latent_parts[1]), "section", 1)
    query_grad = jnp.stack([query_fwd, query_rev], 0)[:, None]
    latent_grad = jnp.stack([latent_fwd, latent_rev], 0)[:, None]
    return (query_grad, latent_grad, weight_grad)


def solution(mesh):
    in_specs = (
        P(None, "section", "dp", "head"),
        P(None, "section", "dp", None),
        P(None, "section", "dp", "head"),
        P(None, "section", "dp"),
        P(None, "section", None, "head"),
    )
    out_specs = (
        P(None, "section", "dp", "head"),
        P(None, "section", ("dp", "head"), None),
        P("section", "dp", "head"),
    )
    return jax.shard_map(body, mesh=mesh, in_specs=in_specs, out_specs=out_specs, check_vma=False)
```

profile of v0, /device:TPU:63, one launch (start us, length us, event | category | flops | bytes accessed | tf_op | source)
XLA Modules:
  0.0 282.4 jit_solution(10947338803245497157)
XLA Ops:
  9.6 2.1 convolution_convert_fusion.2
  16.7 2.5 copy.125
  20.1 2.1 convolution_convert_fusion.3
  28.9 2.4 fusion.36
  32.0 12.1 %all-to-all-start = ((bf16[8,16,576]{2,1,0:T(8,128)(2,1)}), bf16[8,16,576]{2,1,0:T(8,128)(2,1)S(1)}, u32[]{:S(2)}, u32[]{:S(2)}) async-start(bf16[8,16,576]{2,1,0:T(8,128)(2,1)} %pad_maximum_fusion.2), calls=%async_computation | async-start | bytes 327680 | tf_op jit(solution)/shard_map/all_to_all | solution.py:20
  44.1 31.9 %reduce-scatter.9.cloned.1.call-done = bf16[64,2048]{1,0:T(8,128)(2,1)} async-done(((bf16[512,2048]{1,0:T(8,128)(2,1)}), bf16[64,2048]{1,0:T(8,128)(2,1)}) %reduce-scatter.9.cloned.1.call-update) | async-done | bytes 262160
  78.2 24.0 %all-to-all-start.2 = ((bf16[64,16,128]{2,0,1:T(8,128)(2,1)}), bf16[64,16,128]{2,0,1:T(8,128)(2,1)}, u32[]{:S(2)}, u32[]{:S(2)}) async-start(bf16[64,16,128]{2,0,1:T(8,128)(2,1)} %copy.104), calls=%async_computation.2 | async-start | bytes 524288 | tf_op jit(solution)/shard_map/all_to_all | solution.py:124
  103.9 2.5 copy.123
  107.1 1.8 fusion.45
  109.2 2.4 fusion.39
  112.4 32.8 %all-to-all-done.2 = bf16[64,16,128]{2,0,1:T(8,128)(2,1)} async-done(((bf16[64,16,128]{2,0,1:T(8,128)(2,1)}), bf16[64,16,128]{2,0,1:T(8,128)(2,1)}, u32[]{:S(2)}, u32[]{:S(2)}) %all-to-all-start.2) | async-done | bytes 262176 | tf_op jit(solution)/shard_map/all_to_all | solution.py:124
  145.2 3.3 %all-to-all-start.1 = ((bf16[8,16,576]{2,1,0:T(8,128)(2,1)}), bf16[8,16,576]{2,1,0:T(8,128)(2,1)S(1)}, u32[]{:S(2)}, u32[]{:S(2)}) async-start(bf16[8,16,576]{2,1,0:T(8,128)(2,1)} %pad_maximum_fusion.3), calls=%async_computation.1 | async-start | bytes 327680 | tf_op jit(solution)/shard_map/all_to_all | solution.py:20
  150.2 6.7 %all-to-all-done.1 = bf16[8,16,576]{2,1,0:T(8,128)(2,1)S(1)} async-done(((bf16[8,16,576]{2,1,0:T(8,128)(2,1)}), bf16[8,16,576]{2,1,0:T(8,128)(2,1)S(1)}, u32[]{:S(2)}, u32[]{:S(2)}) %all-to-all-start.1) | async-done | bytes 147488 | tf_op jit(solution)/shard_map/all_to_all | solution.py:20
  156.9 9.8 %all-to-all-start.3 = ((bf16[64,16,128]{2,0,1:T(8,128)(2,1)}), bf16[64,16,128]{2,0,1:T(8,128)(2,1)S(1)}, u32[]{:S(2)}, u32[]{:S(2)}) async-start(bf16[64,16,128]{2,0,1:T(8,128)(2,1)} %rev.5), calls=%async_computation.3 | async-start | bytes 524288 | tf_op jit(solution)/shard_map/all_to_all | solution.py:128
  166.8 1.8 fusion.42
  168.6 1.9 fusion.34
  170.7 12.1 %collective-permute-start = (bf16[128,1536]{1,0:T(8,128)(2,1)S(1)}, bf16[128,1536]{1,0:T(8,128)(2,1)S(1)}, u32[]{:S(2)}, u32[]{:S(2)}) collective-permute-start(bf16[128,1536]{1,0:T(8,128)(2,1)S(1)} %copy.81), channel_id=1, source_target_pairs={{64,0},{128,64},{192,128},{256,192},{320,256},{384,320},{448,384},... | collective-permute-start | bytes 1179656 | tf_op jit(solution)/shard_map/ppermute | solution.py:27
  182.8 1.8 fusion.43
  184.7 1.9 fusion.35
  186.8 1.9 collective-permute-start.1
  188.8 13.0 %collective-permute-start.2 = (bf16[16,576]{1,0:T(8,128)(2,1)S(1)}, bf16[16,576]{1,0:T(8,128)(2,1)S(1)}, u32[]{:S(2)}, u32[]{:S(2)}) collective-permute-start(bf16[16,576]{1,0:T(8,128)(2,1)S(1)} %reduce_sum.64), channel_id=1, source_target_pairs={{64,0},{128,64},{192,128},{256,192},{320,256},{384,320},{448,384},... | collective-permute-start | bytes 55304 | tf_op jit(solution)/shard_map/ppermute | solution.py:27
  201.8 1.9 collective-permute-start.3
  203.7 56.2 %collective-permute-done = bf16[128,1536]{1,0:T(8,128)(2,1)S(1)} collective-permute-done((bf16[128,1536]{1,0:T(8,128)(2,1)S(1)}, bf16[128,1536]{1,0:T(8,128)(2,1)S(1)}, u32[]{:S(2)}, u32[]{:S(2)}) %collective-permute-start) | collective-permute-done | bytes 393248 | tf_op jit(solution)/shard_map/ppermute | solution.py:27
  260.0 11.3 %collective-permute-done.1 = bf16[128,1536]{1,0:T(8,128)(2,1)S(1)} collective-permute-done((bf16[128,1536]{1,0:T(8,128)(2,1)S(1)}, bf16[128,1536]{1,0:T(8,128)(2,1)S(1)}, u32[]{:S(2)}, u32[]{:S(2)}) %collective-permute-start.1) | collective-permute-done | bytes 393248 | tf_op jit(solution)/shard_map/ppermute | solution.py:27
  (96 shorter events, 27.3 us)
Async XLA Ops:
  7.2 68.9 %reduce-scatter.9.cloned.1.call-start = ((), (), s32[]{:S(2)}) async-start(), calls=%async_computation.7 | async-start | bytes 2359296
  9.6 6.4 %copy-start = (bf16[128,576]{0,1:T(8,128)(2,1)}, bf16[128,576]{0,1:T(8,128)(2,1)S(1)}, u32[]{:S(2)}) copy-start(bf16[128,576]{0,1:T(8,128)(2,1)S(1)} %get-tuple-element.21) | copy-start | bytes 442372
  9.6 2.3 copy-start.10
  11.7 1.2 copy-start.7
  11.9 2.2 copy-start.3
  14.9 0.9 copy-start.11
  14.9 0.9 copy-start.15
  19.2 0.9 copy-start.1
  19.2 3.1 %copy-start.2 = (bf16[1,1,128,1024]{3,2,1,0:T(8,128)(2,1)S(1)}, bf16[1,1,128,1024]{3,2,1,0:T(8,128)(2,1)}, u32[]{:S(2)}) copy-start(bf16[1,1,128,1024]{3,2,1,0:T(8,128)(2,1)} %get-tuple-element.16) | copy-start | bytes 786436
  22.7 2.0 copy-start.5
  23.7 3.0 %copy-start.13 = (f32[8,128,128]{1,2,0:T(8,128)}, f32[8,128,128]{1,2,0:T(8,128)S(1)}, u32[]{:S(2)}) copy-start(f32[8,128,128]{1,2,0:T(8,128)S(1)} %get-tuple-element.27) | copy-start | bytes 1572868
  32.0 46.2 %all-to-all-start = ((bf16[8,16,576]{2,1,0:T(8,128)(2,1)}), bf16[8,16,576]{2,1,0:T(8,128)(2,1)S(1)}, u32[]{:S(2)}, u32[]{:S(2)}) async-start(bf16[8,16,576]{2,1,0:T(8,128)(2,1)} %pad_maximum_fusion.2), calls=%async_computation | async-start | bytes 327680 | tf_op jit(solution)/shard_map/all_to_all | solution.py:20
  78.2 24.1 %copy-start.8 = (bf16[8,16,576]{2,1,0:T(8,128)(2,1)}, bf16[8,16,576]{2,1,0:T(8,128)(2,1)S(1)}, u32[]{:S(2)}) copy-start(bf16[8,16,576]{2,1,0:T(8,128)(2,1)S(1)} %all-to-all-done) | copy-start | bytes 442372
  78.2 67.0 %all-to-all-start.2 = ((bf16[64,16,128]{2,0,1:T(8,128)(2,1)}), bf16[64,16,128]{2,0,1:T(8,128)(2,1)}, u32[]{:S(2)}, u32[]{:S(2)}) async-start(bf16[64,16,128]{2,0,1:T(8,128)(2,1)} %copy.104), calls=%async_computation.2 | async-start | bytes 524288 | tf_op jit(solution)/shard_map/all_to_all | solution.py:124
  102.2 170.6 %reduce-scatter.7.cloned.1.call-start = ((), (), s32[]{:S(2)}) async-start(), calls=%async_computation.6 | async-start | bytes 2359296
  111.7 56.9 %copy-start.6 = (bf16[128,8,128]{2,1,0:T(8,128)(2,1)S(1)}, bf16[128,8,128]{2,1,0:T(8,128)(2,1)}, u32[]{:S(2)}) copy-start(bf16[128,8,128]{2,1,0:T(8,128)(2,1)} %copy-done.5) | copy-start | bytes 786436
  145.2 11.8 %all-to-all-start.1 = ((bf16[8,16,576]{2,1,0:T(8,128)(2,1)}), bf16[8,16,576]{2,1,0:T(8,128)(2,1)S(1)}, u32[]{:S(2)}, u32[]{:S(2)}) async-start(bf16[8,16,576]{2,1,0:T(8,128)(2,1)} %pad_maximum_fusion.3), calls=%async_computation.1 | async-start | bytes 327680 | tf_op jit(solution)/shard_map/all_to_all | solution.py:20
  156.9 117.2 %all-to-all-start.3 = ((bf16[64,16,128]{2,0,1:T(8,128)(2,1)}), bf16[64,16,128]{2,0,1:T(8,128)(2,1)S(1)}, u32[]{:S(2)}, u32[]{:S(2)}) async-start(bf16[64,16,128]{2,0,1:T(8,128)(2,1)} %rev.5), calls=%async_computation.3 | async-start | bytes 524288 | tf_op jit(solution)/shard_map/all_to_all | solution.py:128
  170.5 14.2 %copy-start.4 = (bf16[128,8,128]{2,1,0:T(8,128)(2,1)S(1)}, bf16[128,8,128]{2,1,0:T(8,128)(2,1)}, u32[]{:S(2)}) copy-start(bf16[128,8,128]{2,1,0:T(8,128)(2,1)} %copy-done.3) | copy-start | bytes 786436
  170.7 89.2 %collective-permute-start = (bf16[128,1536]{1,0:T(8,128)(2,1)S(1)}, bf16[128,1536]{1,0:T(8,128)(2,1)S(1)}, u32[]{:S(2)}, u32[]{:S(2)}) collective-permute-start(bf16[128,1536]{1,0:T(8,128)(2,1)S(1)} %copy.81), channel_id=1, source_target_pairs={{64,0},{128,64},{192,128},{256,192},{320,256},{384,320},{448,384},... | collective-permute-start | bytes 1179656 | tf_op jit(solution)/shard_map/ppermute | solution.py:27
  184.7 4.1 %copy-start.9 = (bf16[8,16,576]{2,1,0:T(8,128)(2,1)S(1)}, bf16[8,16,576]{2,1,0:T(8,128)(2,1)}, u32[]{:S(2)}) copy-start(bf16[8,16,576]{2,1,0:T(8,128)(2,1)} %copy-done.8) | copy-start | bytes 442372
  186.8 84.5 %collective-permute-start.1 = (bf16[128,1536]{1,0:T(8,128)(2,1)S(1)}, bf16[128,1536]{1,0:T(8,128)(2,1)S(1)}, u32[]{:S(2)}, u32[]{:S(2)}) collective-permute-start(bf16[128,1536]{1,0:T(8,128)(2,1)S(1)} %copy.91), channel_id=1, source_target_pairs={{0,64},{64,128},{128,192},{192,256},{256,320},{320,384},{384,448},... | collective-permute-start | bytes 1179656 | tf_op jit(solution)/shard_map/ppermute | solution.py:27
  188.8 83.4 %collective-permute-start.2 = (bf16[16,576]{1,0:T(8,128)(2,1)S(1)}, bf16[16,576]{1,0:T(8,128)(2,1)S(1)}, u32[]{:S(2)}, u32[]{:S(2)}) collective-permute-start(bf16[16,576]{1,0:T(8,128)(2,1)S(1)} %reduce_sum.64), channel_id=1, source_target_pairs={{64,0},{128,64},{192,128},{256,192},{320,256},{384,320},{448,384},... | collective-permute-start | bytes 55304 | tf_op jit(solution)/shard_map/ppermute | solution.py:27
  201.8 70.4 %collective-permute-start.3 = (bf16[16,576]{1,0:T(8,128)(2,1)S(1)}, bf16[16,576]{1,0:T(8,128)(2,1)S(1)}, u32[]{:S(2)}, u32[]{:S(2)}) collective-permute-start(bf16[16,576]{1,0:T(8,128)(2,1)S(1)} %reduce_sum.65), channel_id=1, source_target_pairs={{0,64},{64,128},{128,192},{192,256},{256,320},{320,384},{384,448},... | collective-permute-start | bytes 55304 | tf_op jit(solution)/shard_map/ppermute | solution.py:27
  (3 other events, 2.3 us)
Sparse Core Ops, SparseCore 0:
  19.3 56.7 reduce-scatter.8
  106.5 51.1 reduce-scatter.6
where the time goes:
time: 284 us; the launch traced here: 282 us
  waiting for transfers between devices  139 us (49%)
  starting transfers between devices  78.2 us (28%)
  matrix products  26.9 us (9%)
  local copies, waits for them, and re-layouts  18.8 us (7%)
  between operations  14.6 us (5%)
  other arithmetic  4.85 us (2%)
    ppermute x4, waiting for transfers between devices, from_behind(): return lax.ppermute(block, axis, route)  67.5 us
    all_to_all x1, waiting for transfers between devices, body(): lax.all_to_all(pieces.astype(jnp.bfloat16), 'section', split_axis=1, conc...  32.8 us
    unnamed x4, waiting for transfers between devices  32 us
    ppermute x4, starting transfers between devices, from_behind(): return lax.ppermute(block, axis, route)  28.9 us
    all_to_all x1, starting transfers between devices, body(): lax.all_to_all(pieces.astype(jnp.bfloat16), 'section', split_axis=1, conc...  24 us
    all_to_all x2, starting transfers between devices, summed_on_arrival(): lax.all_to_all(blocks, axis, split_axis=0, concat_axis=0, tiled=True)  15.4 us
    unnamed x45, local copies, waits for them, and re-layouts  10.9 us
    all_to_all x1, starting transfers between devices, body(): lax.all_to_all(flipped.astype(jnp.bfloat16), 'section', split_axis=1, con...  9.82 us
  transfers between devices with their start and end apart: 10, of which 5 were waited for; matrix products, arithmetic and copies ran while one was open for 13% of the time, Pallas kernels for 0%

commit v1 on v0

v1 whole, which is shorter than its diff:
```python
import functools

import jax
import jax.numpy as jnp
from jax import lax
from jax.experimental import pallas as pl
from jax.experimental.pallas import tpu as pltpu
from jax.sharding import PartitionSpec as P

LATENT = 512
ROPE = 64
NOPE = 128
VDIM = 128
QDIM = NOPE + ROPE
KVDIM = NOPE + VDIM
F32 = jnp.float32
BF16 = jnp.bfloat16
NT = (((1,), (1,)), ((), ()))
TN = (((0,), (0,)), ((), ()))
NN = (((1,), (0,)), ((), ()))
COST = pl.CostEstimate(flops=1000, bytes_accessed=1000, transcendentals=0)


def dot(a, b, dims):
    return lax.dot_general(a, b, dims, preferred_element_type=F32)


def attention_kernel(side_ref, q_ref, lat_ref, og_ref, seg_ref, w_ref, qg_ref, kvg_ref, rope_ref, allowed_ref):
    step = pl.program_id(0)
    tokens = q_ref.shape[2]

    @pl.when(step == 0)
    def _():
        across = jnp.broadcast_to(seg_ref[0].astype(F32), (tokens, tokens))
        rows = lax.broadcasted_iota(jnp.int32, (tokens, tokens), 0)
        cols = lax.broadcasted_iota(jnp.int32, (tokens, tokens), 1)
        same = (across == across.T) & (rows >= cols)
        allowed_ref[...] = jnp.where(same, 1.0, 0.0)
        rope_ref[...] = jnp.zeros_like(rope_ref)

    allowed = allowed_ref[...] > 0.5
    latents = lat_ref[0, 0]
    plain, key_rope = latents[:, :LATENT], latents[:, LATENT:]
    kv = dot(plain, w_ref[0, 0], NN).astype(BF16)
    scale = QDIM ** (-0.5)
    for h in range(2):
        query = q_ref[0, 0, :, h * QDIM : (h + 1) * QDIM]
        out_grad = og_ref[0, 0, :, h * VDIM : (h + 1) * VDIM]
        key = kv[:, h * KVDIM : h * KVDIM + NOPE]
        value = kv[:, h * KVDIM + NOPE : (h + 1) * KVDIM]
        key_all = jnp.concatenate([key, key_rope], 1)
        scores = jnp.where(allowed, dot(query, key_all, NT) * scale, -1e30)
        powers = jnp.exp(scores - jnp.max(scores, axis=-1, keepdims=True))
        probs = powers / jnp.sum(powers, axis=-1, keepdims=True)
        grad_probs = dot(out_grad, value, NT)
        delta = jnp.sum(probs * grad_probs, axis=-1, keepdims=True)
        score_grad = (probs * (grad_probs - delta) * scale).astype(BF16)
        qg_ref[:, h * QDIM : (h + 1) * QDIM] = dot(score_grad, key_all, NN).astype(BF16)
        key_grad = dot(score_grad, query, TN)
        value_grad = dot(probs.astype(BF16), out_grad, TN)
        kvg_ref[:, h * KVDIM : h * KVDIM + NOPE] = key_grad[:, :NOPE].astype(BF16)
        kvg_ref[:, h * KVDIM + NOPE : (h + 1) * KVDIM] = value_grad.astype(BF16)
        rope_ref[...] += key_grad[:, NOPE:]


def attention(side, queries, latents, out_grad, segment_ids, up_weight):
    tokens, width = queries.shape[2], up_weight.shape[3]
    pairs = width // (2 * KVDIM)
    return pl.pallas_call(
        attention_kernel,
        grid_spec=pltpu.PrefetchScalarGridSpec(
            num_scalar_prefetch=1,
            grid=(pairs,),
            in_specs=[
                pl.BlockSpec((1, 1, tokens, 2 * QDIM), lambda j, s: (s[0], 0, 0, j)),
                pl.BlockSpec((1, 1, tokens, LATENT + ROPE), lambda j, s: (s[0], 0, 0, 0)),
                pl.BlockSpec((1, 1, tokens, 2 * VDIM), lambda j, s: (s[0], 0, 0, j)),
                pl.BlockSpec((1, 1, tokens), lambda j, s: (s[0], 0, 0)),
                pl.BlockSpec((1, 1, LATENT, 2 * KVDIM), lambda j, s: (s[0], 0, 0, j)),
            ],
            out_specs=[
                pl.BlockSpec((tokens, 2 * QDIM), lambda j, s: (0, j)),
                pl.BlockSpec((tokens, 2 * KVDIM), lambda j, s: (0, j)),
                pl.BlockSpec((tokens, ROPE), lambda j, s: (0, 0)),
            ],
            scratch_shapes=[pltpu.VMEM((tokens, tokens), F32)],
        ),
        out_shape=[
            jax.ShapeDtypeStruct((tokens, pairs * 2 * QDIM), BF16),
            jax.ShapeDtypeStruct((tokens, width), BF16),
            jax.ShapeDtypeStruct((tokens, ROPE), F32),
        ],
        compiler_params=pltpu.CompilerParams(vmem_limit_bytes=58 * 1024 * 1024),
        cost_estimate=COST,
    )(side, queries, latents, out_grad, segment_ids, up_weight)


def partial_kernel(who_ref, kvg0_ref, kvg1_ref, rope0_ref, rope1_ref, lat_ref, w0_ref, w1_ref, keep_ref, send_ref, rows_ref, total_ref):
    step = pl.program_id(0)
    first, core = who_ref[0], who_ref[1]
    shard = keep_ref.shape[1] // 4

    @pl.when(step == 0)
    def _():
        total_ref[...] = jnp.zeros_like(total_ref)

    for i, (kvg_ref, w_ref) in enumerate(((kvg0_ref, w0_ref), (kvg1_ref, w1_ref))):
        kv_grad = kvg_ref[...]
        side = first if i == 0 else 1 - first
        plain = lat_ref[side, 0, :, :LATENT]
        part = dot(plain, kv_grad, TN)
        for y in range(4):
            low = part[(2 * y) * shard : (2 * y + 1) * shard]
            high = part[(2 * y + 1) * shard : (2 * y + 2) * shard]
            keep_ref[i, y * shard : (y + 1) * shard, :] = jnp.where(core == 0, low, high).astype(BF16)
            send_ref[i, y * shard : (y + 1) * shard, :] = jnp.where(core == 0, high, low).astype(BF16)
        total_ref[i] += dot(kv_grad, w_ref[0, 0], NT)

    @pl.when(step == pl.num_programs(0) - 1)
    def _():
        for i, rope_ref in enumerate((rope0_ref, rope1_ref)):
            side = first if i == 0 else 1 - first
            rows_ref[side, :, :LATENT] = total_ref[i].astype(BF16)
            rows_ref[side, :, LATENT:] = rope_ref[...].astype(BF16)


def partials(who, kv_grads, ropes, latents, up_weight):
    tokens, width = kv_grads[0].shape
    cols = 512
    return pl.pallas_call(
        partial_kernel,
        grid_spec=pltpu.PrefetchScalarGridSpec(
            num_scalar_prefetch=1,
            grid=(width // cols,),
            in_specs=[
                pl.BlockSpec((tokens, cols), lambda j, s: (0, j)),
                pl.BlockSpec((tokens, cols), lambda j, s: (0, j)),
                pl.BlockSpec((tokens, ROPE), lambda j, s: (0, 0)),
                pl.BlockSpec((tokens, ROPE), lambda j, s: (0, 0)),
                pl.BlockSpec(latents.shape, lambda j, s: (0, 0, 0, 0)),
                pl.BlockSpec((1, 1, LATENT, cols), lambda j, s: (s[0], 0, 0, j)),
                pl.BlockSpec((1, 1, LATENT, cols), lambda j, s: (1 - s[0], 0, 0, j)),
            ],
            out_specs=[
                pl.BlockSpec((2, LATENT // 2, cols), lambda j, s: (0, 0, j)),
                pl.BlockSpec((2, LATENT // 2, cols), lambda j, s: (0, 0, j)),
                pl.BlockSpec((2, tokens, LATENT + ROPE), lambda j, s: (0, 0, 0)),
            ],
            scratch_shapes=[pltpu.VMEM((2, tokens, LATENT), F32)],
        ),
        out_shape=[
            jax.ShapeDtypeStruct((2, LATENT // 2, width), BF16),
            jax.ShapeDtypeStruct((2, LATENT // 2, width), BF16),
            jax.ShapeDtypeStruct((2, tokens, LATENT + ROPE), BF16),
        ],
        compiler_params=pltpu.CompilerParams(vmem_limit_bytes=32 * 1024 * 1024),
        cost_estimate=COST,
    )(who, *kv_grads, *ropes, latents, up_weight, up_weight)


def pair_kernel(y_ref, keep_ref, came_ref, *out_refs):
    shard = out_refs[0].shape[1]
    side = pl.program_id(0)
    for out_ref, (zero, one) in zip(out_refs, ((0, 0), (2, 1), (3, 2), (1, 3))):
        ahead = jnp.where(side == 0, zero, one)
        rows = pl.ds(pl.multiple_of(lax.rem(y_ref[0] + ahead, 4) * shard, shard), shard)
        out_ref[0] = (keep_ref[0, rows, :].astype(F32) + came_ref[0, rows, :].astype(F32)).astype(BF16)


def pair_sums(y, keep, came):
    sides, rows, width = keep.shape
    cols = width // 2
    return pl.pallas_call(
        pair_kernel,
        grid_spec=pltpu.PrefetchScalarGridSpec(
            num_scalar_prefetch=1,
            grid=(sides, width // cols),
            in_specs=[pl.BlockSpec((1, rows, cols), lambda i, j, s: (i, 0, j))] * 2,
            out_specs=[pl.BlockSpec((1, rows // 4, cols), lambda i, j, s: (i, 0, j))] * 4,
        ),
        out_shape=[jax.ShapeDtypeStruct((sides, rows // 4, width), BF16)] * 4,
        compiler_params=pltpu.CompilerParams(vmem_limit_bytes=32 * 1024 * 1024),
        cost_estimate=COST,
    )(y, keep, came)


def placed_kernel(first_ref, one_ref, other_ref, out_ref):
    out_ref[first_ref[0], 0] = one_ref[...]
    out_ref[1 - first_ref[0], 0] = other_ref[...]


def placed(first, arrived):
    rows, width = arrived[0].shape
    cols = width // 4
    return pl.pallas_call(
        placed_kernel,
        grid_spec=pltpu.PrefetchScalarGridSpec(
            num_scalar_prefetch=1,
            grid=(width // cols,),
            in_specs=[pl.BlockSpec((rows, cols), lambda j, s: (0, j))] * 2,
            out_specs=pl.BlockSpec((2, 1, rows, cols), lambda j, s: (0, 0, 0, j)),
        ),
        out_shape=jax.ShapeDtypeStruct((2, 1, rows, width), BF16),
        cost_estimate=COST,
    )(first[None], *arrived)


def total_kernel(after_ref, forward_ref, mirrored_ref, out_ref):
    out_ref[0] = forward_ref[...] + mirrored_ref[...].astype(F32)


def total_of(after, forward, mirrored):
    rows, width = forward.shape
    cols = width // 4
    return pl.pallas_call(
        total_kernel,
        grid=(width // cols,),
        in_specs=[pl.BlockSpec(memory_space=pl.ANY)] + [pl.BlockSpec((rows, cols), lambda j: (0, j))] * 2,
        out_specs=pl.BlockSpec((1, rows, cols), lambda j: (0, 0, j)),
        out_shape=jax.ShapeDtypeStruct((1, rows, width), F32),
        cost_estimate=COST,
    )(after, forward, mirrored)


def relay(block, away):
    sections, heads = lax.axis_size("section"), lax.axis_size("head")
    route = []
    for s in range(sections):
        for h in range(heads):
            there = s - 1 if (h + away) % 2 == 0 else s + 1
            if 0 <= there < sections:
                route.append((s * heads + h, there * heads + h))
    return lax.ppermute(block, ("section", "head"), route)


def sum_over_replicas(first, core, y, kv_grads, ropes, latents, up_weight):
    keep, send, rows = partials(jnp.stack([first, core]), kv_grads, ropes, latents, up_weight)
    came = lax.ppermute(send, "dp", [(i, i ^ 1) for i in range(8)])
    own, up, down, rest = pair_sums(y[None], keep, came)
    above, below = [(i, (i + 2) % 8) for i in range(8)], [(i, (i - 2) % 8) for i in range(8)]
    from_below = lax.ppermute(up, "dp", above).astype(F32)
    from_above = lax.ppermute(down, "dp", below).astype(F32)
    up = (rest[0].astype(F32) + from_below[0]).astype(BF16)
    down = (rest[1].astype(F32) + from_above[1]).astype(BF16)
    up = lax.ppermute(up, "dp", above).astype(F32)
    down = lax.ppermute(down, "dp", below).astype(F32)
    total = (own[0].astype(F32) + from_above[0] + up, own[1].astype(F32) + from_below[1] + down)
    forward = jnp.where(first == 0, total[0], total[1])
    reverse = jnp.where(first == 0, total[1], total[0]).astype(BF16)

    head = lax.axis_index("head")
    part = rows.reshape(2, 8, rows.shape[1] // 8, LATENT + ROPE)
    for bit in range(3):
        part = part.reshape(2, part.shape[1] // 2, 2, *part.shape[2:])
        mine = lax.rem(lax.div(head, 1 << bit), 2)
        sent = jnp.where(mine == 0, part[:, :, 1], part[:, :, 0]).astype(BF16)
        kept = jnp.where(mine == 0, part[:, :, 0], part[:, :, 1]).astype(F32)
        part = kept + lax.ppermute(sent, "head", [(i, i ^ (1 << bit)) for i in range(8)]).astype(F32)
    part = part[:, 0].astype(BF16)
    return forward, reverse, jnp.where(first == 0, part[0], part[1]), jnp.where(first == 0, part[1], part[0])


def body(queries, latents, out_grad, segment_ids, up_weight):
    head, dp = lax.axis_index("head"), lax.axis_index("dp")
    first = lax.rem(head, 2).astype(jnp.int32)
    core, y = lax.rem(dp, 2).astype(jnp.int32), lax.div(dp, 2).astype(jnp.int32)
    sections = lax.axis_size("section")

    results, arrived = [], []
    for i in range(2):
        side = (first if i == 0 else 1 - first)[None]
        results.append(attention(side, queries, latents, out_grad, segment_ids, up_weight))
        arrived.append(relay(results[i][0], i))

    sums = functools.partial(sum_over_replicas, first, core, y)
    operands = ([r[1] for r in results], [r[2] for r in results], latents, up_weight)
    nothing = jax.tree.map(lambda a: jnp.zeros(a.shape, a.dtype), jax.eval_shape(sums, *operands))
    forward, reverse, *parts = lax.cond(segment_ids[0, 0, 0] >= 0, sums, lambda *_: nothing, *operands)

    mirrored = lax.ppermute(reverse, "section", [(i, sections - 1 - i) for i in range(sections)])
    query_grad = placed(first, arrived)
    weight_grad = total_of(query_grad, forward, mirrored)
    latent_arrived = [relay(parts[i], i) for i in range(2)]

    def in_order(pair):
        return jnp.stack([jnp.where(first == 0, pair[0], pair[1]), jnp.where(first == 0, pair[1], pair[0])], 0)[:, None]

    return (query_grad, in_order(latent_arrived), weight_grad)


def solution(mesh):
    in_specs = (
        P(None, "section", "dp", "head"),
        P(None, "section", "dp", None),
        P(None, "section", "dp", "head"),
        P(None, "section", "dp"),
        P(None, "section", None, "head"),
    )
    out_specs = (
        P(None, "section", "dp", "head"),
        P(None, "section", ("dp", "head"), None),
        P("section", "dp", "head"),
    )
    return jax.shard_map(body, mesh=mesh, in_specs=in_specs, out_specs=out_specs, check_vma=False)
```

time: 284 us -> 215 us (0.76)
  the two profiles are of different devices: /device:TPU:63 before, /device:TPU:257 now
where the time goes in v1:
time: 215 us; the launch traced here: 213 us
  waiting for transfers between devices  104 us (48%)
  starting transfers between devices  67.8 us (32%)
  Pallas kernels  32 us (15%)
  other arithmetic  3.77 us (2%)
  local copies, waits for them, and re-layouts  3.29 us (2%)
    ppermute x3, waiting for transfers between devices, sum_over_replicas(): lax.ppermute(sent, 'head', [(i, i ^ 1 << bit) for i in range(8)])  48.4 us
    ppermute x1, waiting for transfers between devices, body(): lax.ppermute(reverse, 'section', [(i, sections - 1 - i) for i in range(se...  45 us
    ppermute x4, starting transfers between devices, relay(): return lax.ppermute(block, ('section', 'head'), route)  31.3 us
    pallas_call x2, Pallas kernels, attention(): pl.pallas_call(attention_kernel, grid_spec=pltpu.PrefetchScalarGridSpec(n...  15 us
    ppermute x3, starting transfers between devices, sum_over_replicas(): lax.ppermute(sent, 'head', [(i, i ^ 1 << bit) for i in range(8)])  11.5 us
    ppermute x1, starting transfers between devices, body(): lax.ppermute(reverse, 'section', [(i, sections - 1 - i) for i in range(se...  10.2 us
    pallas_call x1, Pallas kernels, partials(): pl.pallas_call(partial_kernel, grid_spec=pltpu.PrefetchScalarGridSpec(num...  6.63 us
    ppermute x1, waiting for transfers between devices, sum_over_replicas(): from_below = lax.ppermute(up, 'dp', above).astype(F32)  4.83 us
  transfers between devices with their start and end apart: 13, of which 6 were waited for; matrix products, arithmetic and copies ran while one was open for 2% of the time, Pallas kernels for 10%

profile of v1, /device:TPU:257, one launch (start us, length us, event | category | flops | bytes accessed | tf_op | source)
XLA Modules:
  0.0 212.6 jit_solution(8111985291748270948)
XLA Ops:
  2.5 7.6 %shard_map.77 = (bf16[128,1536]{1,0:T(8,128)(2,1)}, bf16[128,2048]{1,0:T(8,128)(2,1)S(1)}, f32[128,64]{1,0:T(8,128)S(1)}) custom-call(s32[1]{0:T(128)} %bitcast.26.side_ref, bf16[2,1,128,1536]{3,2,1,0:T(8,128)(2,1)} %q_ref.3, bf16[2,1,128,576]{3,2,1,0:T(8,128)(2,1)} %copy.26.lat_ref, bf16[2,1,128,1024]{3,2,1,0:T(8,128)(2,1)} %og_ref.3, ...), custom_call_target="tpu_custom_call" | custom-call | flops 1000 | bytes 1000 | tf_op jit(solution)/shard_map/pallas_call | solution.py:69
  10.1 15.4 %collective-permute-start.9 = (bf16[128,1536]{1,0:T(8,128)(2,1)}, bf16[128,1536]{1,0:T(8,128)(2,1)}, u32[]{:S(2)}, u32[]{:S(2)}) collective-permute-start(bf16[128,1536]{1,0:T(8,128)(2,1)} %get-tuple-element.64), channel_id=1, source_target_pairs={{0,64},{2,66},{4,68},{6,70},{64,128},{65,1},{66,130},{67,3},{68,13... | collective-permute-start | bytes 1179656 | tf_op jit(solution)/shard_map/ppermute | solution.py:233
  25.5 7.4 %shard_map.76 = (bf16[128,1536]{1,0:T(8,128)(2,1)}, bf16[128,2048]{1,0:T(8,128)(2,1)}, f32[128,64]{1,0:T(8,128)S(1)}) custom-call(s32[1]{0:T(128)} %bitcast.25.side_ref.first_ref, bf16[2,1,128,1536]{3,2,1,0:T(8,128)(2,1)} %q_ref.3, bf16[2,1,128,576]{3,2,1,0:T(8,128)(2,1)} %copy.26.lat_ref, bf16[2,1,128,1024]{3,2,1,0:T(8,128)(2,1)} %og_ref.3, ...), custom_call_target="tpu_custom_call" | custom-call | flops 1000 | bytes 1000 | tf_op jit(solution)/shard_map/pallas_call | solution.py:69
  33.0 1.9 collective-permute-start.8
  36.1 99.5 %conditional.1 = (f32[64,2048]{1,0:T(8,128)}, bf16[64,2048]{1,0:T(8,128)(2,1)}, bf16[16,576]{1,0:T(8,128)(2,1)}, bf16[16,576]{1,0:T(8,128)(2,1)}) conditional(s32[]{:T(128)} %bitcast.27, () %tuple.17, (s32[]{:T(128)}, s32[]{:T(128)}, bf16[128,2048]{1,0:T(8,128)(2,1)}, bf16[128,2048]{1,0:T(8,128)(2,1)S(1)}, f32[128,64]{1,0:T(8,128)S(1)}, ...), branch_computations={%region_0.0_spmd, %region_1.2_spmd} | conditional | flops 3381241 | bytes 26753736 | solution.py:278
  36.4 6.6 %branch_1_fun.2 = (bf16[2,256,2048]{2,1,0:T(8,128)(2,1)S(1)}, bf16[2,256,2048]{2,1,0:T(8,128)(2,1)}, bf16[2,128,576]{2,1,0:T(8,128)(2,1)S(1)}) custom-call(s32[2]{0:T(128)S(1)} %pad_add_fusion.who_ref, bf16[128,2048]{1,0:T(8,128)(2,1)} %get-tuple-element.37.kvg0_ref, bf16[128,2048]{1,0:T(8,128)(2,1)S(1)} %get-tuple-element.38.kvg1_ref, ...), custom_call_target="tpu_custom_call" | custom-call | flops 1000 | bytes 1000 | tf_op jit(solution)/shard_map/cond/branch_1_fun/pallas_call | solution.py:130
  43.0 2.9 %collective-permute-start = (bf16[2,256,2048]{2,1,0:T(8,128)(2,1)}, bf16[2,256,2048]{2,1,0:T(8,128)(2,1)}, u32[]{:S(2)}, u32[]{:S(2)}) collective-permute-start(bf16[2,256,2048]{2,1,0:T(8,128)(2,1)} %get-tuple-element.44), channel_id=1, source_target_pairs={{0,8},{8,0},{16,24},{24,16},{32,40},{40,32},{48,56},{56,48},{1,9},... | collective-permute-start | bytes 6291464 | tf_op jit(solution)/shard_map/cond/branch_1_fun/ppermute | solution.py:238
  45.9 2.6 %collective-permute-start.5 = (bf16[2,4,16,576]{3,2,1,0:T(8,128)(2,1)S(1)}, bf16[2,4,16,576]{3,2,1,0:T(8,128)(2,1)S(1)}, u32[]{:S(2)}, u32[]{:S(2)}) collective-permute-start(bf16[2,4,16,576]{3,2,1,0:T(8,128)(2,1)S(1)} %select_bitcast_fusion), channel_id=1, source_target_pairs={{0,1},{1,0},{2,3},{3,2},{4,5},{5,4},{6,7},{7,6},{8,9},{9,8},{10,11... | collective-permute-start | bytes 442376 | tf_op jit(solution)/shard_map/cond/branch_1_fun/ppermute | solution.py:258
  48.6 48.4 %collective-permute-done.5 = bf16[2,4,16,576]{3,2,1,0:T(8,128)(2,1)S(1)} collective-permute-done((bf16[2,4,16,576]{3,2,1,0:T(8,128)(2,1)S(1)}, bf16[2,4,16,576]{3,2,1,0:T(8,128)(2,1)S(1)}, u32[]{:S(2)}, u32[]{:S(2)}) %collective-permute-start.5) | collective-permute-done | bytes 147488 | tf_op jit(solution)/shard_map/cond/branch_1_fun/ppermute | solution.py:258
  97.1 3.4 %collective-permute-start.6 = (bf16[2,2,16,576]{3,2,1,0:T(8,128)(2,1)S(1)}, bf16[2,2,16,576]{3,2,1,0:T(8,128)(2,1)}, u32[]{:S(2)}, u32[]{:S(2)}) collective-permute-start(bf16[2,2,16,576]{3,2,1,0:T(8,128)(2,1)S(1)} %fusion.11), channel_id=1, source_target_pairs={{0,2},{1,3},{2,0},{3,1},{4,6},{5,7},{6,4},{7,5},{8,10},{9,11},{10,... | collective-permute-start | bytes 221192 | tf_op jit(solution)/shard_map/cond/branch_1_fun/ppermute | solution.py:258
  100.5 3.9 %branch_1_fun.3 = (bf16[2,64,2048]{2,1,0:T(8,128)(2,1)S(1)}, bf16[2,64,2048]{2,1,0:T(8,128)(2,1)}, bf16[2,64,2048]{2,1,0:T(8,128)(2,1)}, bf16[2,64,2048]{2,1,0:T(8,128)(2,1)S(1)}) custom-call(s32[1]{0:T(128)} %bitcast.y_ref, bf16[2,256,2048]{2,1,0:T(8,128)(2,1)S(1)} %get-tuple-element.43.keep_ref, bf16[2,256,2048]{2,1,0:T(8,128)(2,1)} %collective-permute-done.came_ref), custom_call_target="tpu_custom_call" | custom-call | flops 1000 | bytes 1000 | tf_op jit(solution)/shard_map/cond/branch_1_fun/pallas_call | solution.py:173
  104.4 4.6 %collective-permute-start.1 = (bf16[2,64,2048]{2,1,0:T(8,128)(2,1)}, bf16[2,64,2048]{2,1,0:T(8,128)(2,1)S(1)}, u32[]{:S(2)}, u32[]{:S(2)}) collective-permute-start(bf16[2,64,2048]{2,1,0:T(8,128)(2,1)} %get-tuple-element.46), channel_id=1, source_target_pairs={{0,48},{8,56},{16,0},{24,8},{32,16},{40,24},{48,32},{56,40},{1,49}... | collective-permute-start | bytes 1572872 | tf_op jit(solution)/shard_map/cond/branch_1_fun/ppermute | solution.py:242
  109.0 1.9 collective-permute-start.2
  111.9 5.5 %collective-permute-start.7 = (bf16[2,1,16,576]{3,2,0,1:T(8,128)(2,1)S(1)}, bf16[2,1,16,576]{3,2,0,1:T(8,128)(2,1)S(1)}, u32[]{:S(2)}, u32[]{:S(2)}) collective-permute-start(bf16[2,1,16,576]{3,2,0,1:T(8,128)(2,1)S(1)} %fusion.15), channel_id=1, source_target_pairs={{0,4},{1,5},{2,6},{3,7},{4,0},{5,1},{6,2},{7,3},{8,12},{9,13},{10,... | collective-permute-start | bytes 110600 | tf_op jit(solution)/shard_map/cond/branch_1_fun/ppermute | solution.py:258
  119.2 4.8 %collective-permute-done.2 = bf16[2,64,2048]{2,1,0:T(8,128)(2,1)S(1)} collective-permute-done((bf16[2,64,2048]{2,1,0:T(8,128)(2,1)}, bf16[2,64,2048]{2,1,0:T(8,128)(2,1)S(1)}, u32[]{:S(2)}, u32[]{:S(2)}) %collective-permute-start.2) | collective-permute-done | bytes 524320 | tf_op jit(solution)/shard_map/cond/branch_1_fun/ppermute | solution.py:241
  124.2 1.9 collective-permute-start.4
  126.2 3.4 %collective-permute-start.3 = (bf16[64,2048]{1,0:T(8,128)(2,1)S(1)}, bf16[64,2048]{1,0:T(8,128)(2,1)S(1)}, u32[]{:S(2)}, u32[]{:S(2)}) collective-permute-start(bf16[64,2048]{1,0:T(8,128)(2,1)S(1)} %get-tuple-element.92), channel_id=1, source_target_pairs={{0,16},{8,24},{16,32},{24,40},{32,48},{40,56},{48,0},{56,8},{1,17}... | collective-permute-start | bytes 786440 | tf_op jit(solution)/shard_map/cond/branch_1_fun/ppermute | solution.py:245
  131.4 3.1 %collective-permute-done.3 = bf16[64,2048]{1,0:T(8,128)(2,1)S(1)} collective-permute-done((bf16[64,2048]{1,0:T(8,128)(2,1)S(1)}, bf16[64,2048]{1,0:T(8,128)(2,1)S(1)}, u32[]{:S(2)}, u32[]{:S(2)}) %collective-permute-start.3) | collective-permute-done | bytes 262176 | tf_op jit(solution)/shard_map/cond/branch_1_fun/ppermute | solution.py:245
  135.6 2.3 %collective-permute-start.10 = (bf16[16,576]{1,0:T(8,128)(2,1)}, bf16[16,576]{1,0:T(8,128)(2,1)S(1)}, u32[]{:S(2)}, u32[]{:S(2)}) collective-permute-start(bf16[16,576]{1,0:T(8,128)(2,1)} %get-tuple-element.69), channel_id=1, source_target_pairs={{1,65},{3,67},{5,69},{7,71},{64,0},{65,129},{66,2},{67,131},{68,4}... | collective-permute-start | bytes 55304 | tf_op jit(solution)/shard_map/ppermute | solution.py:233
  137.9 11.7 %collective-permute-start.11 = (bf16[16,576]{1,0:T(8,128)(2,1)}, bf16[16,576]{1,0:T(8,128)(2,1)S(1)}, u32[]{:S(2)}, u32[]{:S(2)}) collective-permute-start(bf16[16,576]{1,0:T(8,128)(2,1)} %get-tuple-element.70), channel_id=1, source_target_pairs={{0,64},{2,66},{4,68},{6,70},{64,128},{65,1},{66,130},{67,3},{68,13... | collective-permute-start | bytes 55304 | tf_op jit(solution)/shard_map/ppermute | solution.py:233
  149.6 10.2 %collective-permute-start.12 = (bf16[64,2048]{1,0:T(8,128)(2,1)}, bf16[64,2048]{1,0:T(8,128)(2,1)S(1)}, u32[]{:S(2)}, u32[]{:S(2)}) collective-permute-start(bf16[64,2048]{1,0:T(8,128)(2,1)} %get-tuple-element.72), channel_id=1, source_target_pairs={{0,960},{64,896},{128,832},{192,768},{256,704},{320,640},{384,576}... | collective-permute-start | bytes 786440 | tf_op jit(solution)/shard_map/ppermute | solution.py:280
  160.5 3.3 %shard_map.78.after_ref = bf16[2,1,128,1536]{3,2,1,0:T(8,128)(2,1)} custom-call(s32[1]{0:T(128)} %bitcast.25.side_ref.first_ref, bf16[128,1536]{1,0:T(8,128)(2,1)} %collective-permute-done.8.one_ref, bf16[128,1536]{1,0:T(8,128)(2,1)} %collective-permute-done.9.other_ref), custom_call_target="tpu_custom_call" | custom-call | flops 1000 | bytes 1000 | tf_op jit(solution)/shard_map/pallas_call | solution.py:195
  163.8 45.0 %collective-permute-done.12.mirrored_ref = bf16[64,2048]{1,0:T(8,128)(2,1)S(1)} collective-permute-done((bf16[64,2048]{1,0:T(8,128)(2,1)}, bf16[64,2048]{1,0:T(8,128)(2,1)S(1)}, u32[]{:S(2)}, u32[]{:S(2)}) %collective-permute-start.12) | collective-permute-done | bytes 262176 | tf_op jit(solution)/shard_map/ppermute | solution.py:280
  209.5 3.2 %shard_map.79 = f32[1,64,2048]{2,1,0:T(8,128)} custom-call(bf16[2,1,128,1536]{3,2,1,0:T(8,128)(2,1)} %shard_map.78.after_ref, f32[64,2048]{1,0:T(8,128)} %get-tuple-element.71.forward_ref, bf16[64,2048]{1,0:T(8,128)(2,1)} %copy-done.2), custom_call_target="tpu_custom_call" | custom-call | flops 1000 | bytes 1000 | tf_op jit(solution)/shard_map/pallas_call | solution.py:215
  (34 shorter events, 9.9 us)
Async XLA Ops:
  2.5 23.0 %copy-start = (bf16[2,1,512,2048]{3,2,1,0:T(8,128)(2,1)S(1)}, bf16[2,1,512,2048]{3,2,1,0:T(8,128)(2,1)}, u32[]{:S(2)}) copy-start(bf16[2,1,512,2048]{3,2,1,0:T(8,128)(2,1)} %w_ref.3) | copy-start | bytes 12582916
  10.1 150.4 %collective-permute-start.9 = (bf16[128,1536]{1,0:T(8,128)(2,1)}, bf16[128,1536]{1,0:T(8,128)(2,1)}, u32[]{:S(2)}, u32[]{:S(2)}) collective-permute-start(bf16[128,1536]{1,0:T(8,128)(2,1)} %get-tuple-element.64), channel_id=1, source_target_pairs={{0,64},{2,66},{4,68},{6,70},{64,128},{65,1},{66,130},{67,3},{68,13... | collective-permute-start | bytes 1179656 | tf_op jit(solution)/shard_map/ppermute | solution.py:233
  25.5 9.4 %copy-start.3 = (s32[2,1,128]{2,1,0:T(1,128)S(1)}, s32[2,1,128]{2,1,0:T(1,128)}, u32[]{:S(2)}) copy-start(s32[2,1,128]{2,1,0:T(1,128)} %seg_ref.3) | copy-start | bytes 3076
  25.5 10.5 %copy-start.1 = (bf16[2,1,128,576]{2,3,1,0:T(8,128)(2,1)S(1)}, bf16[2,1,128,576]{2,3,1,0:T(8,128)(2,1)}, u32[]{:S(2)}) copy-start(bf16[2,1,128,576]{2,3,1,0:T(8,128)(2,1)} %param.8) | copy-start | bytes 884740
  33.0 127.5 %collective-permute-start.8 = (bf16[128,1536]{1,0:T(8,128)(2,1)}, bf16[128,1536]{1,0:T(8,128)(2,1)}, u32[]{:S(2)}, u32[]{:S(2)}) collective-permute-start(bf16[128,1536]{1,0:T(8,128)(2,1)} %get-tuple-element.63), channel_id=1, source_target_pairs={{1,65},{3,67},{5,69},{7,71},{64,0},{65,129},{66,2},{67,131},{68,4}... | collective-permute-start | bytes 1179656 | tf_op jit(solution)/shard_map/ppermute | solution.py:233
  43.0 57.5 %collective-permute-start = (bf16[2,256,2048]{2,1,0:T(8,128)(2,1)}, bf16[2,256,2048]{2,1,0:T(8,128)(2,1)}, u32[]{:S(2)}, u32[]{:S(2)}) collective-permute-start(bf16[2,256,2048]{2,1,0:T(8,128)(2,1)} %get-tuple-element.44), channel_id=1, source_target_pairs={{0,8},{8,0},{16,24},{24,16},{32,40},{40,32},{48,56},{56,48},{1,9},... | collective-permute-start | bytes 6291464 | tf_op jit(solution)/shard_map/cond/branch_1_fun/ppermute | solution.py:238
  45.9 51.1 %collective-permute-start.5 = (bf16[2,4,16,576]{3,2,1,0:T(8,128)(2,1)S(1)}, bf16[2,4,16,576]{3,2,1,0:T(8,128)(2,1)S(1)}, u32[]{:S(2)}, u32[]{:S(2)}) collective-permute-start(bf16[2,4,16,576]{3,2,1,0:T(8,128)(2,1)S(1)} %select_bitcast_fusion), channel_id=1, source_target_pairs={{0,1},{1,0},{2,3},{3,2},{4,5},{5,4},{6,7},{7,6},{8,9},{9,8},{10,11... | collective-permute-start | bytes 442376 | tf_op jit(solution)/shard_map/cond/branch_1_fun/ppermute | solution.py:258
  97.1 13.9 %collective-permute-start.6 = (bf16[2,2,16,576]{3,2,1,0:T(8,128)(2,1)S(1)}, bf16[2,2,16,576]{3,2,1,0:T(8,128)(2,1)}, u32[]{:S(2)}, u32[]{:S(2)}) collective-permute-start(bf16[2,2,16,576]{3,2,1,0:T(8,128)(2,1)S(1)} %fusion.11), channel_id=1, source_target_pairs={{0,2},{1,3},{2,0},{3,1},{4,6},{5,7},{6,4},{7,5},{8,10},{9,11},{10,... | collective-permute-start | bytes 221192 | tf_op jit(solution)/shard_map/cond/branch_1_fun/ppermute | solution.py:258
  104.4 14.7 %collective-permute-start.1 = (bf16[2,64,2048]{2,1,0:T(8,128)(2,1)}, bf16[2,64,2048]{2,1,0:T(8,128)(2,1)S(1)}, u32[]{:S(2)}, u32[]{:S(2)}) collective-permute-start(bf16[2,64,2048]{2,1,0:T(8,128)(2,1)} %get-tuple-element.46), channel_id=1, source_target_pairs={{0,48},{8,56},{16,0},{24,8},{32,16},{40,24},{48,32},{56,40},{1,49}... | collective-permute-start | bytes 1572872 | tf_op jit(solution)/shard_map/cond/branch_1_fun/ppermute | solution.py:242
  109.0 15.0 %collective-permute-start.2 = (bf16[2,64,2048]{2,1,0:T(8,128)(2,1)}, bf16[2,64,2048]{2,1,0:T(8,128)(2,1)S(1)}, u32[]{:S(2)}, u32[]{:S(2)}) collective-permute-start(bf16[2,64,2048]{2,1,0:T(8,128)(2,1)} %get-tuple-element.48), channel_id=1, source_target_pairs={{0,16},{8,24},{16,32},{24,40},{32,48},{40,56},{48,0},{56,8},{1,17}... | collective-permute-start | bytes 1572872 | tf_op jit(solution)/shard_map/cond/branch_1_fun/ppermute | solution.py:241
  111.9 17.6 %collective-permute-start.7 = (bf16[2,1,16,576]{3,2,0,1:T(8,128)(2,1)S(1)}, bf16[2,1,16,576]{3,2,0,1:T(8,128)(2,1)S(1)}, u32[]{:S(2)}, u32[]{:S(2)}) collective-permute-start(bf16[2,1,16,576]{3,2,0,1:T(8,128)(2,1)S(1)} %fusion.15), channel_id=1, source_target_pairs={{0,4},{1,5},{2,6},{3,7},{4,0},{5,1},{6,2},{7,3},{8,12},{9,13},{10,... | collective-permute-start | bytes 110600 | tf_op jit(solution)/shard_map/cond/branch_1_fun/ppermute | solution.py:258
  124.2 7.1 %collective-permute-start.4 = (bf16[64,2048]{1,0:T(8,128)(2,1)S(1)}, bf16[64,2048]{1,0:T(8,128)(2,1)S(1)}, u32[]{:S(2)}, u32[]{:S(2)}) collective-permute-start(bf16[64,2048]{1,0:T(8,128)(2,1)S(1)} %get-tuple-element.91), channel_id=1, source_target_pairs={{0,48},{8,56},{16,0},{24,8},{32,16},{40,24},{48,32},{56,40},{1,49}... | collective-permute-start | bytes 786440 | tf_op jit(solution)/shard_map/cond/branch_1_fun/ppermute | solution.py:246
  126.2 8.3 %collective-permute-start.3 = (bf16[64,2048]{1,0:T(8,128)(2,1)S(1)}, bf16[64,2048]{1,0:T(8,128)(2,1)S(1)}, u32[]{:S(2)}, u32[]{:S(2)}) collective-permute-start(bf16[64,2048]{1,0:T(8,128)(2,1)S(1)} %get-tuple-element.92), channel_id=1, source_target_pairs={{0,16},{8,24},{16,32},{24,40},{32,48},{40,56},{48,0},{56,8},{1,17}... | collective-permute-start | bytes 786440 | tf_op jit(solution)/shard_map/cond/branch_1_fun/ppermute | solution.py:245
  135.6 24.3 %collective-permute-start.10 = (bf16[16,576]{1,0:T(8,128)(2,1)}, bf16[16,576]{1,0:T(8,128)(2,1)S(1)}, u32[]{:S(2)}, u32[]{:S(2)}) collective-permute-start(bf16[16,576]{1,0:T(8,128)(2,1)} %get-tuple-element.69), channel_id=1, source_target_pairs={{1,65},{3,67},{5,69},{7,71},{64,0},{65,129},{66,2},{67,131},{68,4}... | collective-permute-start | bytes 55304 | tf_op jit(solution)/shard_map/ppermute | solution.py:233
  137.9 22.0 %collective-permute-start.11 = (bf16[16,576]{1,0:T(8,128)(2,1)}, bf16[16,576]{1,0:T(8,128)(2,1)S(1)}, u32[]{:S(2)}, u32[]{:S(2)}) collective-permute-start(bf16[16,576]{1,0:T(8,128)(2,1)} %get-tuple-element.70), channel_id=1, source_target_pairs={{0,64},{2,66},{4,68},{6,70},{64,128},{65,1},{66,130},{67,3},{68,13... | collective-permute-start | bytes 55304 | tf_op jit(solution)/shard_map/ppermute | solution.py:233
  149.6 59.2 %collective-permute-start.12 = (bf16[64,2048]{1,0:T(8,128)(2,1)}, bf16[64,2048]{1,0:T(8,128)(2,1)S(1)}, u32[]{:S(2)}, u32[]{:S(2)}) collective-permute-start(bf16[64,2048]{1,0:T(8,128)(2,1)} %get-tuple-element.72), channel_id=1, source_target_pairs={{0,960},{64,896},{128,832},{192,768},{256,704},{320,640},{384,576}... | collective-permute-start | bytes 786440 | tf_op jit(solution)/shard_map/ppermute | solution.py:280
  208.8 0.7 copy-start.2

commit v2 on v1

--- a/solution.py
+++ b/solution.py
@@ -25,7 +25,7 @@
     return lax.dot_general(a, b, dims, preferred_element_type=F32)
 
 
-def attention_kernel(side_ref, q_ref, lat_ref, og_ref, seg_ref, w_ref, qg_ref, kvg_ref, rope_ref, allowed_ref):
+def attention_kernel(side_ref, q_ref, lat_ref, og_ref, seg_ref, w_ref, qg_ref, kvg_ref, rows_ref, allowed_ref, rope_ref, total_ref):
     step = pl.program_id(0)
     tokens = q_ref.shape[2]
 
@@ -37,6 +37,7 @@
         same = (across == across.T) & (rows >= cols)
         allowed_ref[...] = jnp.where(same, 1.0, 0.0)
         rope_ref[...] = jnp.zeros_like(rope_ref)
+        total_ref[...] = jnp.zeros_like(total_ref)
 
     allowed = allowed_ref[...] > 0.5
     latents = lat_ref[0, 0]
@@ -61,6 +62,12 @@
         kvg_ref[:, h * KVDIM : h * KVDIM + NOPE] = key_grad[:, :NOPE].astype(BF16)
         kvg_ref[:, h * KVDIM + NOPE : (h + 1) * KVDIM] = value_grad.astype(BF16)
         rope_ref[...] += key_grad[:, NOPE:]
+    total_ref[...] += dot(kvg_ref[...], w_ref[0, 0], NT)
+
+    @pl.when(step == pl.num_programs(0) - 1)
+    def _():
+        rows_ref[:, :LATENT] = total_ref[...].astype(BF16)
+        rows_ref[:, LATENT:] = rope_ref[...].astype(BF16)
 
 
 def attention(side, queries, latents, out_grad, segment_ids, up_weight):
@@ -81,50 +88,38 @@
             out_specs=[
                 pl.BlockSpec((tokens, 2 * QDIM), lambda j, s: (0, j)),
                 pl.BlockSpec((tokens, 2 * KVDIM), lambda j, s: (0, j)),
-                pl.BlockSpec((tokens, ROPE), lambda j, s: (0, 0)),
-            ],
-            scratch_shapes=[pltpu.VMEM((tokens, tokens), F32)],
+                pl.BlockSpec((tokens, LATENT + ROPE), lambda j, s: (0, 0)),
+            ],
+            scratch_shapes=[
+                pltpu.VMEM((tokens, tokens), F32),
+                pltpu.VMEM((tokens, ROPE), F32),
+                pltpu.VMEM((tokens, LATENT), F32),
+            ],
         ),
         out_shape=[
             jax.ShapeDtypeStruct((tokens, pairs * 2 * QDIM), BF16),
             jax.ShapeDtypeStruct((tokens, width), BF16),
-            jax.ShapeDtypeStruct((tokens, ROPE), F32),
+            jax.ShapeDtypeStruct((tokens, LATENT + ROPE), BF16),
         ],
         compiler_params=pltpu.CompilerParams(vmem_limit_bytes=58 * 1024 * 1024),
         cost_estimate=COST,
     )(side, queries, latents, out_grad, segment_ids, up_weight)
 
 
-def partial_kernel(who_ref, kvg0_ref, kvg1_ref, rope0_ref, rope1_ref, lat_ref, w0_ref, w1_ref, keep_ref, send_ref, rows_ref, total_ref):
-    step = pl.program_id(0)
+def partial_kernel(who_ref, kvg0_ref, kvg1_ref, lat_ref, keep_ref, send_ref):
     first, core = who_ref[0], who_ref[1]
     shard = keep_ref.shape[1] // 4
-
-    @pl.when(step == 0)
-    def _():
-        total_ref[...] = jnp.zeros_like(total_ref)
-
-    for i, (kvg_ref, w_ref) in enumerate(((kvg0_ref, w0_ref), (kvg1_ref, w1_ref))):
-        kv_grad = kvg_ref[...]
+    for i, kvg_ref in enumerate((kvg0_ref, kvg1_ref)):
         side = first if i == 0 else 1 - first
-        plain = lat_ref[side, 0, :, :LATENT]
-        part = dot(plain, kv_grad, TN)
+        part = dot(lat_ref[side, 0, :, :LATENT], kvg_ref[...], TN)
         for y in range(4):
             low = part[(2 * y) * shard : (2 * y + 1) * shard]
             high = part[(2 * y + 1) * shard : (2 * y + 2) * shard]
             keep_ref[i, y * shard : (y + 1) * shard, :] = jnp.where(core == 0, low, high).astype(BF16)
             send_ref[i, y * shard : (y + 1) * shard, :] = jnp.where(core == 0, high, low).astype(BF16)
-        total_ref[i] += dot(kv_grad, w_ref[0, 0], NT)
-
-    @pl.when(step == pl.num_programs(0) - 1)
-    def _():
-        for i, rope_ref in enumerate((rope0_ref, rope1_ref)):
-            side = first if i == 0 else 1 - first
-            rows_ref[side, :, :LATENT] = total_ref[i].astype(BF16)
-            rows_ref[side, :, LATENT:] = rope_ref[...].astype(BF16)
-
-
-def partials(who, kv_grads, ropes, latents, up_weight):
+
+
+def partials(who, kv_grads, latents):
     tokens, width = kv_grads[0].shape
     cols = 512
     return pl.pallas_call(
@@ -135,27 +130,20 @@
             in_specs=[
                 pl.BlockSpec((tokens, cols), lambda j, s: (0, j)),
                 pl.BlockSpec((tokens, cols), lambda j, s: (0, j)),
-                pl.BlockSpec((tokens, ROPE), lambda j, s: (0, 0)),
-                pl.BlockSpec((tokens, ROPE), lambda j, s: (0, 0)),
                 pl.BlockSpec(latents.shape, lambda j, s: (0, 0, 0, 0)),
-                pl.BlockSpec((1, 1, LATENT, cols), lambda j, s: (s[0], 0, 0, j)),
-                pl.BlockSpec((1, 1, LATENT, cols), lambda j, s: (1 - s[0], 0, 0, j)),
             ],
             out_specs=[
                 pl.BlockSpec((2, LATENT // 2, cols), lambda j, s: (0, 0, j)),
                 pl.BlockSpec((2, LATENT // 2, cols), lambda j, s: (0, 0, j)),
-                pl.BlockSpec((2, tokens, LATENT + ROPE), lambda j, s: (0, 0, 0)),
-            ],
-            scratch_shapes=[pltpu.VMEM((2, tokens, LATENT), F32)],
+            ],
         ),
         out_shape=[
             jax.ShapeDtypeStruct((2, LATENT // 2, width), BF16),
             jax.ShapeDtypeStruct((2, LATENT // 2, width), BF16),
-            jax.ShapeDtypeStruct((2, tokens, LATENT + ROPE), BF16),
         ],
         compiler_params=pltpu.CompilerParams(vmem_limit_bytes=32 * 1024 * 1024),
         cost_estimate=COST,
-    )(who, *kv_grads, *ropes, latents, up_weight, up_weight)
+    )(who, *kv_grads, latents)
 
 
 def pair_kernel(y_ref, keep_ref, came_ref, *out_refs):
@@ -184,6 +172,22 @@
     )(y, keep, came)
 
 
+def held_kernel(after_ref, *refs):
+    pass
+
+
+def held(after, arrays):
+    anywhere = pl.BlockSpec(memory_space=pl.ANY)
+    return pl.pallas_call(
+        held_kernel,
+        in_specs=[anywhere] * (1 + len(arrays)),
+        out_specs=[anywhere] * len(arrays),
+        out_shape=[jax.ShapeDtypeStruct(a.shape, a.dtype) for a in arrays],
+        input_output_aliases={i + 1: i for i in range(len(arrays))},
+        cost_estimate=COST,
+    )(after, *arrays)
+
+
 def placed_kernel(first_ref, one_ref, other_ref, out_ref):
     out_ref[first_ref[0], 0] = one_ref[...]
     out_ref[1 - first_ref[0], 0] = other_ref[...]
@@ -201,25 +205,41 @@
             out_specs=pl.BlockSpec((2, 1, rows, cols), lambda j, s: (0, 0, 0, j)),
         ),
         out_shape=jax.ShapeDtypeStruct((2, 1, rows, width), BF16),
+        compiler_params=pltpu.CompilerParams(vmem_limit_bytes=16 * 1024 * 1024),
         cost_estimate=COST,
     )(first[None], *arrived)
 
 
-def total_kernel(after_ref, forward_ref, mirrored_ref, out_ref):
+def total_kernel(first_ref, after_ref, forward_ref, mirrored_ref, one_ref, other_ref, out_ref, rows_ref):
     out_ref[0] = forward_ref[...] + mirrored_ref[...].astype(F32)
-
-
-def total_of(after, forward, mirrored):
+    rows_ref[first_ref[0], 0] = one_ref[...]
+    rows_ref[1 - first_ref[0], 0] = other_ref[...]
+
+
+def total_of(first, after, forward, mirrored, latent_rows):
     rows, width = forward.shape
-    cols = width // 4
+    cols = width // 2
+    few = latent_rows[0].shape
     return pl.pallas_call(
         total_kernel,
-        grid=(width // cols,),
-        in_specs=[pl.BlockSpec(memory_space=pl.ANY)] + [pl.BlockSpec((rows, cols), lambda j: (0, j))] * 2,
-        out_specs=pl.BlockSpec((1, rows, cols), lambda j: (0, 0, j)),
-        out_shape=jax.ShapeDtypeStruct((1, rows, width), F32),
-        cost_estimate=COST,
-    )(after, forward, mirrored)
+        grid_spec=pltpu.PrefetchScalarGridSpec(
+            num_scalar_prefetch=1,
+            grid=(width // cols,),
+            in_specs=[pl.BlockSpec(memory_space=pl.ANY)]
+            + [pl.BlockSpec((rows, cols), lambda j, s: (0, j))] * 2
+            + [pl.BlockSpec(few, lambda j, s: (0, 0))] * 2,
+            out_specs=[
+                pl.BlockSpec((1, rows, cols), lambda j, s: (0, 0, j)),
+                pl.BlockSpec((2, 1, *few), lambda j, s: (0, 0, 0, 0)),
+            ],
+        ),
+        out_shape=[
+            jax.ShapeDtypeStruct((1, rows, width), F32),
+            jax.ShapeDtypeStruct((2, 1, *few), BF16),
+        ],
+        compiler_params=pltpu.CompilerParams(vmem_limit_bytes=16 * 1024 * 1024),
+        cost_estimate=COST,
+    )(first[None], after, forward, mirrored, *latent_rows)
 
 
 def relay(block, away):
@@ -233,8 +253,7 @@
     return lax.ppermute(block, ("section", "head"), route)
 
 
-def sum_over_replicas(first, core, y, kv_grads, ropes, latents, up_weight):
-    keep, send, rows = partials(jnp.stack([first, core]), kv_grads, ropes, latents, up_weight)
+def sum_over_replicas(first, y, keep, send):
     came = lax.ppermute(send, "dp", [(i, i ^ 1) for i in range(8)])
     own, up, down, rest = pair_sums(y[None], keep, came)
     above, below = [(i, (i + 2) % 8) for i in range(8)], [(i, (i - 2) % 8) for i in range(8)]
@@ -247,17 +266,23 @@
     total = (own[0].astype(F32) + from_above[0] + up, own[1].astype(F32) + from_below[1] + down)
     forward = jnp.where(first == 0, total[0], total[1])
     reverse = jnp.where(first == 0, total[1], total[0]).astype(BF16)
-
+    return forward, reverse
+
+
+def sum_over_heads(part):
     head = lax.axis_index("head")
-    part = rows.reshape(2, 8, rows.shape[1] // 8, LATENT + ROPE)
+    part = part.reshape(2, 8, part.shape[1] // 8, LATENT + ROPE)
     for bit in range(3):
         part = part.reshape(2, part.shape[1] // 2, 2, *part.shape[2:])
         mine = lax.rem(lax.div(head, 1 << bit), 2)
         sent = jnp.where(mine == 0, part[:, :, 1], part[:, :, 0]).astype(BF16)
         kept = jnp.where(mine == 0, part[:, :, 0], part[:, :, 1]).astype(F32)
         part = kept + lax.ppermute(sent, "head", [(i, i ^ (1 << bit)) for i in range(8)]).astype(F32)
-    part = part[:, 0].astype(BF16)
-    return forward, reverse, jnp.where(first == 0, part[0], part[1]), jnp.where(first == 0, part[1], part[0])
+    return part[:, 0].astype(BF16)
+
+
+def in_order(first, one, other):
+    return jnp.stack([jnp.where(first == 0, one, other), jnp.where(first == 0, other, one)], 0)
 
 
 def body(queries, latents, out_grad, segment_ids, up_weight):
@@ -266,26 +291,27 @@
     core, y = lax.rem(dp, 2).astype(jnp.int32), lax.div(dp, 2).astype(jnp.int32)
     sections = lax.axis_size("section")
 
-    results, arrived = [], []
-    for i in range(2):
-        side = (first if i == 0 else 1 - first)[None]
-        results.append(attention(side, queries, latents, out_grad, segment_ids, up_weight))
-        arrived.append(relay(results[i][0], i))
-
-    sums = functools.partial(sum_over_replicas, first, core, y)
-    operands = ([r[1] for r in results], [r[2] for r in results], latents, up_weight)
-    nothing = jax.tree.map(lambda a: jnp.zeros(a.shape, a.dtype), jax.eval_shape(sums, *operands))
-    forward, reverse, *parts = lax.cond(segment_ids[0, 0, 0] >= 0, sums, lambda *_: nothing, *operands)
+    query_grads, kv_grads, rows = zip(
+        *[
+            attention((first if i == 0 else 1 - first)[None], queries, latents, out_grad, segment_ids, up_weight)
+            for i in range(2)
+        ]
+    )
+    part = sum_over_heads(in_order(first, *rows))
+    part = in_order(first, part[0], part[1])
+    keep, send = partials(jnp.stack([first, core]), kv_grads, latents)
+    query_grads = held(part, query_grads)
+    arrived = [relay(query_grads[i], i) for i in range(2)]
+    latent_here = [relay(part[i], i) for i in range(2)]
+
+    sums = functools.partial(sum_over_replicas, first, y)
+    nothing = jax.tree.map(lambda a: jnp.zeros(a.shape, a.dtype), jax.eval_shape(sums, keep, send))
+    forward, reverse = lax.cond(segment_ids[0, 0, 0] >= 0, sums, lambda *_: nothing, keep, send)
 
     mirrored = lax.ppermute(reverse, "section", [(i, sections - 1 - i) for i in range(sections)])
     query_grad = placed(first, arrived)
-    weight_grad = total_of(query_grad, forward, mirrored)
-    latent_arrived = [relay(parts[i], i) for i in range(2)]
-
-    def in_order(pair):
-        return jnp.stack([jnp.where(first == 0, pair[0], pair[1]), jnp.where(first == 0, pair[1], pair[0])], 0)[:, None]
-
-    return (query_grad, in_order(latent_arrived), weight_grad)
+    weight_grad, latent_grad = total_of(first, query_grad, forward, mirrored, latent_here)
+    return (query_grad, latent_grad, weight_grad)
 
 
 def solution(mesh):

time: 215 us -> 190 us (0.88)
  waiting for transfers between devices: 104 us -> 72.3 us
  starting transfers between devices: 67.8 us -> 80 us
  Pallas kernels: 32 us -> 26.4 us
    ppermute x3, waiting for transfers between devices: 48.4 us -> 6.97 us  [sum_over_heads(): lax.ppermute(sent, 'head', [(i, i ^ 1 << bit) for i in range(8)])]
    ppermute x1, waiting for transfers between devices: 1.66 us -> 8.99 us  [sum_over_replicas(): from_above = lax.ppermute(down, 'dp', below).astype(F32)]
    ppermute x3, starting transfers between devices: 11.5 us -> 17.4 us  [sum_over_heads(): lax.ppermute(sent, 'head', [(i, i ^ 1 << bit) for i in range(8)])]
    ppermute x1, starting transfers between devices: 10.2 us -> 14.5 us  [body(): lax.ppermute(reverse, 'section', [(i, sections - 1 - i) for i in range(se...]
    ppermute x1, waiting for transfers between devices: 0.01 us -> 3.97 us  [sum_over_replicas(): came = lax.ppermute(send, 'dp', [(i, i ^ 1) for i in range(8)])]
    ppermute x1, waiting for transfers between devices: 45 us -> 41.2 us  [body(): lax.ppermute(reverse, 'section', [(i, sections - 1 - i) for i in range(se...]
    ppermute x1, starting transfers between devices: 2.86 us -> 6.03 us  [sum_over_replicas(): came = lax.ppermute(send, 'dp', [(i, i ^ 1) for i in range(8)])]
    pallas_call x1, Pallas kernels: 6.63 us -> 4.05 us  [partials(): pl.pallas_call(partial_kernel, grid_spec=pltpu.PrefetchScalarGridSpec(num...]
  transfers between devices with their start and end apart: 13 -> 13, of which waited for: 6 -> 9; matrix products, arithmetic and copies ran while one was open for 2% -> 2% of each run, Pallas kernels for 10% -> 4%
where the time goes in v2:
time: 190 us; the launch traced here: 189 us
  starting transfers between devices  80 us (42%)
  waiting for transfers between devices  72.3 us (38%)
  Pallas kernels  26.4 us (14%)
  other arithmetic  5.05 us (3%)
  local copies, waits for them, and re-layouts  3.55 us (2%)
    ppermute x1, waiting for transfers between devices, body(): lax.ppermute(reverse, 'section', [(i, sections - 1 - i) for i in range(se...  41.2 us
    ppermute x4, starting transfers between devices, relay(): return lax.ppermute(block, ('section', 'head'), route)  30.2 us
    ppermute x3, starting transfers between devices, sum_over_heads(): lax.ppermute(sent, 'head', [(i, i ^ 1 << bit) for i in range(8)])  17.4 us
    pallas_call x2, Pallas kernels, attention(): pl.pallas_call(attention_kernel, grid_spec=pltpu.PrefetchScalarGridSpec(n...  16.3 us
    ppermute x1, starting transfers between devices, body(): lax.ppermute(reverse, 'section', [(i, sections - 1 - i) for i in range(se...  14.5 us
    ppermute x1, waiting for transfers between devices, sum_over_replicas(): from_above = lax.ppermute(down, 'dp', below).astype(F32)  8.99 us
    ppermute x3, waiting for transfers between devices, sum_over_heads(): lax.ppermute(sent, 'head', [(i, i ^ 1 << bit) for i in range(8)])  6.97 us
    ppermute x1, starting transfers between devices, sum_over_replicas(): came = lax.ppermute(send, 'dp', [(i, i ^ 1) for i in range(8)])  6.03 us
  transfers between devices with their start and end apart: 13, of which 9 were waited for; matrix products, arithmetic and copies ran while one was open for 2% of the time, Pallas kernels for 4%

profile of v2, /device:TPU:257, one launch (start us, length us, event | category | flops | bytes accessed | tf_op | source)
XLA Modules:
  0.0 188.9 jit_solution(1663603292922101506)
XLA Ops:
  2.5 8.1 %shard_map.77 = (bf16[128,1536]{1,0:T(8,128)(2,1)}, bf16[128,2048]{1,0:T(8,128)(2,1)}, bf16[128,576]{1,0:T(8,128)(2,1)}) custom-call(s32[1]{0:T(128)} %bitcast.6.side_ref, bf16[2,1,128,1536]{3,2,1,0:T(8,128)(2,1)} %q_ref.3, bf16[2,1,128,576]{3,2,1,0:T(8,128)(2,1)} %copy.18.lat_ref, bf16[2,1,128,1024]{3,2,1,0:T(8,128)(2,1)} %og_ref.3, s32[2,1,128]{2,1,0:T(1,128)} %seg_ref.3, ...), custom_call_target="tpu_custom_call" | custom-call | flops 1000 | bytes 1000 | tf_op jit(solution)/shard_map/pallas_call | solution.py:76
  10.6 8.2 %shard_map.76 = (bf16[128,1536]{1,0:T(8,128)(2,1)}, bf16[128,2048]{1,0:T(8,128)(2,1)}, bf16[128,576]{1,0:T(8,128)(2,1)}) custom-call(s32[1]{0:T(128)} %bitcast.5.side_ref.first_ref, bf16[2,1,128,1536]{3,2,1,0:T(8,128)(2,1)} %q_ref.3, bf16[2,1,128,576]{3,2,1,0:T(8,128)(2,1)} %copy.18.lat_ref, bf16[2,1,128,1024]{3,2,1,0:T(8,128)(2,1)} %og_ref.3, ...), custom_call_target="tpu_custom_call" | custom-call | flops 1000 | bytes 1000 | tf_op jit(solution)/shard_map/pallas_call | solution.py:76
  19.9 3.7 %collective-permute-start.5 = (bf16[2,4,16,576]{3,2,1,0:T(8,128)(2,1)S(1)}, bf16[2,4,16,576]{3,2,1,0:T(8,128)(2,1)S(1)}, u32[]{:S(2)}, u32[]{:S(2)}) collective-permute-start(bf16[2,4,16,576]{3,2,1,0:T(8,128)(2,1)S(1)} %select_bitcast_fusion), channel_id=1, source_target_pairs={{0,1},{1,0},{2,3},{3,2},{4,5},{5,4},{6,7},{7,6},{8,9},{9,8},{10,11... | collective-permute-start | bytes 442376 | tf_op jit(solution)/shard_map/ppermute | solution.py:280
  23.6 3.8 %collective-permute-done.5 = bf16[2,4,16,576]{3,2,1,0:T(8,128)(2,1)S(1)} collective-permute-done((bf16[2,4,16,576]{3,2,1,0:T(8,128)(2,1)S(1)}, bf16[2,4,16,576]{3,2,1,0:T(8,128)(2,1)S(1)}, u32[]{:S(2)}, u32[]{:S(2)}) %collective-permute-start.5) | collective-permute-done | bytes 147488 | tf_op jit(solution)/shard_map/ppermute | solution.py:280
  27.5 4.9 %collective-permute-start.6 = (bf16[2,2,16,576]{3,2,0,1:T(8,128)(2,1)S(1)}, bf16[2,2,16,576]{3,2,0,1:T(8,128)(2,1)S(1)}, u32[]{:S(2)}, u32[]{:S(2)}) collective-permute-start(bf16[2,2,16,576]{3,2,0,1:T(8,128)(2,1)S(1)} %fusion.12), channel_id=1, source_target_pairs={{0,2},{1,3},{2,0},{3,1},{4,6},{5,7},{6,4},{7,5},{8,10},{9,11},{10,... | collective-permute-start | bytes 221192 | tf_op jit(solution)/shard_map/ppermute | solution.py:280
  34.3 8.8 %collective-permute-start.7 = (bf16[2,1,16,576]{3,2,1,0:T(8,128)(2,1)S(1)}, bf16[2,1,16,576]{3,2,1,0:T(8,128)(2,1)S(1)}, u32[]{:S(2)}, u32[]{:S(2)}) collective-permute-start(bf16[2,1,16,576]{3,2,1,0:T(8,128)(2,1)S(1)} %fusion.14), channel_id=1, source_target_pairs={{0,4},{1,5},{2,6},{3,7},{4,0},{5,1},{6,2},{7,3},{8,12},{9,13},{10,... | collective-permute-start | bytes 110600 | tf_op jit(solution)/shard_map/ppermute | solution.py:280
  47.1 14.3 %collective-permute-start.9 = (bf16[128,1536]{1,0:T(8,128)(2,1)}, bf16[128,1536]{1,0:T(8,128)(2,1)S(1)}, u32[]{:S(2)}, u32[]{:S(2)}) collective-permute-start(bf16[128,1536]{1,0:T(8,128)(2,1)} %get-tuple-element.46), channel_id=1, source_target_pairs={{0,64},{2,66},{4,68},{6,70},{64,128},{65,1},{66,130},{67,3},{68,13... | collective-permute-start | bytes 1179656 | tf_op jit(solution)/shard_map/ppermute | solution.py:253
  61.5 4.0 %shard_map.80 = (bf16[2,256,2048]{2,1,0:T(8,128)(2,1)}, bf16[2,256,2048]{2,1,0:T(8,128)(2,1)}) custom-call(s32[2]{0:T(128)S(1)} %pad_add_fusion.who_ref, bf16[128,2048]{1,0:T(8,128)(2,1)S(1)} %copy-done.3, bf16[128,2048]{1,0:T(8,128)(2,1)S(1)} %copy-done.2, bf16[2,1,128,576]{3,2,1,0:T(8,128)(2,1)S(1)} %copy-done), custom_call_target="tpu_custom_call" | custom-call | flops 1000 | bytes 1000 | tf_op jit(solution)/shard_map/pallas_call | solution.py:125
  66.7 48.0 %conditional.1 = (f32[64,2048]{1,0:T(8,128)}, bf16[64,2048]{1,0:T(8,128)(2,1)}) conditional(s32[]{:T(128)} %bitcast.20, () %tuple.16, (s32[]{:T(128)}, s32[]{:T(128)}, pred[]{:T(512)}, bf16[2,256,2048]{2,1,0:T(8,128)(2,1)}, bf16[2,256,2048]{2,1,0:T(8,128)(2,1)}) %tuple.17), branch_computations={%region_0.1_spmd, %region_1.2_spmd} | conditional | flops 2753516 | bytes 22807788 | solution.py:309
  66.7 6.0 %collective-permute-start = (bf16[2,256,2048]{2,1,0:T(8,128)(2,1)}, bf16[2,256,2048]{2,1,0:T(8,128)(2,1)S(1)}, u32[]{:S(2)}, u32[]{:S(2)}) collective-permute-start(bf16[2,256,2048]{2,1,0:T(8,128)(2,1)} %get-tuple-element.19), channel_id=1, source_target_pairs={{0,8},{8,0},{16,24},{24,16},{32,40},{40,32},{48,56},{56,48},{1,9},... | collective-permute-start | bytes 6291464 | tf_op jit(solution)/shard_map/cond/branch_1_fun/ppermute | solution.py:257
  72.7 4.0 %collective-permute-done.came_ref = bf16[2,256,2048]{2,1,0:T(8,128)(2,1)S(1)} collective-permute-done((bf16[2,256,2048]{2,1,0:T(8,128)(2,1)}, bf16[2,256,2048]{2,1,0:T(8,128)(2,1)S(1)}, u32[]{:S(2)}, u32[]{:S(2)}) %collective-permute-start) | collective-permute-done | bytes 2097184 | tf_op jit(solution)/shard_map/cond/branch_1_fun/ppermute | solution.py:257
  76.7 2.7 %branch_1_fun.1 = (bf16[2,64,2048]{2,1,0:T(8,128)(2,1)S(1)}, bf16[2,64,2048]{2,1,0:T(8,128)(2,1)S(1)}, bf16[2,64,2048]{2,1,0:T(8,128)(2,1)S(1)}, bf16[2,64,2048]{2,1,0:T(8,128)(2,1)S(1)}) custom-call(s32[1]{0:T(128)} %bitcast.y_ref, bf16[2,256,2048]{2,1,0:T(8,128)(2,1)} %get-tuple-element.18.keep_ref, bf16[2,256,2048]{2,1,0:T(8,128)(2,1)S(1)} %collective-permute-done.came_ref), custom_call_target="tpu_custom_call" | custom-call | flops 1000 | bytes 1000 | tf_op jit(solution)/shard_map/cond/branch_1_fun/pallas_call | solution.py:161
  79.4 4.6 %collective-permute-start.1 = (bf16[2,64,2048]{2,1,0:T(8,128)(2,1)S(1)}, bf16[2,64,2048]{2,1,0:T(8,128)(2,1)S(1)}, u32[]{:S(2)}, u32[]{:S(2)}) collective-permute-start(bf16[2,64,2048]{2,1,0:T(8,128)(2,1)S(1)} %get-tuple-element.21), channel_id=1, source_target_pairs={{0,48},{8,56},{16,0},{24,8},{32,16},{40,24},{48,32},{56,40},{1,49}... | collective-permute-start | bytes 1572872 | tf_op jit(solution)/shard_map/cond/branch_1_fun/ppermute | solution.py:261
  84.1 1.9 %collective-permute-start.2 = (bf16[2,64,2048]{2,1,0:T(8,128)(2,1)S(1)}, bf16[2,64,2048]{2,1,0:T(8,128)(2,1)S(1)}, u32[]{:S(2)}, u32[]{:S(2)}) collective-permute-start(bf16[2,64,2048]{2,1,0:T(8,128)(2,1)S(1)} %get-tuple-element.23), channel_id=1, source_target_pairs={{0,16},{8,24},{16,32},{24,40},{32,48},{40,56},{48,0},{56,8},{1,17}... | collective-permute-start | bytes 1572872 | tf_op jit(solution)/shard_map/cond/branch_1_fun/ppermute | solution.py:260
  86.0 9.0 %collective-permute-done.1 = bf16[2,64,2048]{2,1,0:T(8,128)(2,1)S(1)} collective-permute-done((bf16[2,64,2048]{2,1,0:T(8,128)(2,1)S(1)}, bf16[2,64,2048]{2,1,0:T(8,128)(2,1)S(1)}, u32[]{:S(2)}, u32[]{:S(2)}) %collective-permute-start.1) | collective-permute-done | bytes 524320 | tf_op jit(solution)/shard_map/cond/branch_1_fun/ppermute | solution.py:261
  95.1 4.9 %collective-permute-done.2 = bf16[2,64,2048]{2,1,0:T(8,128)(2,1)S(1)} collective-permute-done((bf16[2,64,2048]{2,1,0:T(8,128)(2,1)S(1)}, bf16[2,64,2048]{2,1,0:T(8,128)(2,1)S(1)}, u32[]{:S(2)}, u32[]{:S(2)}) %collective-permute-start.2) | collective-permute-done | bytes 524320 | tf_op jit(solution)/shard_map/cond/branch_1_fun/ppermute | solution.py:260
  102.9 3.4 %collective-permute-start.3 = (bf16[64,2048]{1,0:T(8,128)(2,1)}, bf16[64,2048]{1,0:T(8,128)(2,1)}, u32[]{:S(2)}, u32[]{:S(2)}) collective-permute-start(bf16[64,2048]{1,0:T(8,128)(2,1)} %get-tuple-element.58), channel_id=1, source_target_pairs={{0,16},{8,24},{16,32},{24,40},{32,48},{40,56},{48,0},{56,8},{1,17}... | collective-permute-start | bytes 786440 | tf_op jit(solution)/shard_map/cond/branch_1_fun/ppermute | solution.py:264
  106.3 3.2 %collective-permute-done.4 = bf16[64,2048]{1,0:T(8,128)(2,1)} collective-permute-done((bf16[64,2048]{1,0:T(8,128)(2,1)}, bf16[64,2048]{1,0:T(8,128)(2,1)}, u32[]{:S(2)}, u32[]{:S(2)}) %collective-permute-start.4) | collective-permute-done | bytes 262176 | tf_op jit(solution)/shard_map/cond/branch_1_fun/ppermute | solution.py:265
  109.5 3.1 %collective-permute-done.3 = bf16[64,2048]{1,0:T(8,128)(2,1)} collective-permute-done((bf16[64,2048]{1,0:T(8,128)(2,1)}, bf16[64,2048]{1,0:T(8,128)(2,1)}, u32[]{:S(2)}, u32[]{:S(2)}) %collective-permute-start.3) | collective-permute-done | bytes 262176 | tf_op jit(solution)/shard_map/cond/branch_1_fun/ppermute | solution.py:264
  112.6 2.1 %select_convert_fusion = (bf16[64,2048]{1,0:T(8,128)(2,1)}, f32[64,2048]{1,0:T(8,128)}) fusion(pred[]{:T(512)S(6)} %eq.0, bf16[64,2048]{1,0:T(8,128)(2,1)} %collective-permute-done.3, f32[2,64,2048]{2,1,0:T(8,128)S(1)} %convert_element_type.64, bf16[2,64,2048]{2,1,0:T(8,128)(2,1)S(1)} %get-tuple-element.20, bf16[64,2048]{1,0:T(8,128)(2,1)} %collective-permute-done.4, ...), kind=kLoop, calls=%fused_computation.10 | loop fusion | flops 1441792 | bytes 2883585 | tf_op jit(solution)/shard_map/cond/branch_1_fun/convert_element_type | solution.py:268
  114.7 14.5 %collective-permute-start.10 = (bf16[64,2048]{1,0:T(8,128)(2,1)}, bf16[64,2048]{1,0:T(8,128)(2,1)S(1)}, u32[]{:S(2)}, u32[]{:S(2)}) collective-permute-start(bf16[64,2048]{1,0:T(8,128)(2,1)} %get-tuple-element.52), channel_id=1, source_target_pairs={{0,960},{64,896},{128,832},{192,768},{256,704},{320,640},{384,576}... | collective-permute-start | bytes 786440 | tf_op jit(solution)/shard_map/ppermute | solution.py:311
  129.3 1.9 %collective-permute-start.12 = (bf16[16,576]{1,0:T(8,128)(2,1)S(1)}, bf16[16,576]{1,0:T(8,128)(2,1)S(1)}, u32[]{:S(2)}, u32[]{:S(2)}) collective-permute-start(bf16[16,576]{1,0:T(8,128)(2,1)S(1)} %get-tuple-element.63), channel_id=1, source_target_pairs={{0,64},{2,66},{4,68},{6,70},{64,128},{65,1},{66,130},{67,3},{68,13... | collective-permute-start | bytes 55304 | tf_op jit(solution)/shard_map/ppermute | solution.py:253
  131.2 12.1 %collective-permute-start.11 = (bf16[16,576]{1,0:T(8,128)(2,1)S(1)}, bf16[16,576]{1,0:T(8,128)(2,1)S(1)}, u32[]{:S(2)}, u32[]{:S(2)}) collective-permute-start(bf16[16,576]{1,0:T(8,128)(2,1)S(1)} %get-tuple-element.64), channel_id=1, source_target_pairs={{1,65},{3,67},{5,69},{7,71},{64,0},{65,129},{66,2},{67,131},{68,4}... | collective-permute-start | bytes 55304 | tf_op jit(solution)/shard_map/ppermute | solution.py:253
  144.8 41.2 %collective-permute-done.10.mirrored_ref = bf16[64,2048]{1,0:T(8,128)(2,1)S(1)} collective-permute-done((bf16[64,2048]{1,0:T(8,128)(2,1)}, bf16[64,2048]{1,0:T(8,128)(2,1)S(1)}, u32[]{:S(2)}, u32[]{:S(2)}) %collective-permute-start.10) | collective-permute-done | bytes 262176 | tf_op jit(solution)/shard_map/ppermute | solution.py:311
  (39 shorter events, 16.9 us)
Async XLA Ops:
  10.6 8.2 %copy-start.4 = (bf16[128,576]{1,0:T(8,128)(2,1)S(1)}, bf16[128,576]{1,0:T(8,128)(2,1)}, u32[]{:S(2)}) copy-start(bf16[128,576]{1,0:T(8,128)(2,1)} %get-tuple-element.42) | copy-start | bytes 442372
  19.8 41.7 %copy-start = (bf16[2,1,128,576]{3,2,1,0:T(8,128)(2,1)S(1)}, bf16[2,1,128,576]{3,2,1,0:T(8,128)(2,1)}, u32[]{:S(2)}) copy-start(bf16[2,1,128,576]{3,2,1,0:T(8,128)(2,1)} %copy.18.lat_ref) | copy-start | bytes 884740
  19.8 41.7 %copy-start.2 = (bf16[128,2048]{1,0:T(8,128)(2,1)S(1)}, bf16[128,2048]{1,0:T(8,128)(2,1)}, u32[]{:S(2)}) copy-start(bf16[128,2048]{1,0:T(8,128)(2,1)} %get-tuple-element.48.kvg1_ref) | copy-start | bytes 1572868
  19.8 41.7 %copy-start.3 = (bf16[128,2048]{1,0:T(8,128)(2,1)S(1)}, bf16[128,2048]{1,0:T(8,128)(2,1)}, u32[]{:S(2)}) copy-start(bf16[128,2048]{1,0:T(8,128)(2,1)} %get-tuple-element.47.kvg0_ref) | copy-start | bytes 1572868
  19.9 7.5 %collective-permute-start.5 = (bf16[2,4,16,576]{3,2,1,0:T(8,128)(2,1)S(1)}, bf16[2,4,16,576]{3,2,1,0:T(8,128)(2,1)S(1)}, u32[]{:S(2)}, u32[]{:S(2)}) collective-permute-start(bf16[2,4,16,576]{3,2,1,0:T(8,128)(2,1)S(1)} %select_bitcast_fusion), channel_id=1, source_target_pairs={{0,1},{1,0},{2,3},{3,2},{4,5},{5,4},{6,7},{7,6},{8,9},{9,8},{10,11... | collective-permute-start | bytes 442376 | tf_op jit(solution)/shard_map/ppermute | solution.py:280
  27.4 38.1 %copy-start.5 = (s32[2,1,128]{2,1,0:T(1,128)S(1)}, s32[2,1,128]{2,1,0:T(1,128)}, u32[]{:S(2)}) copy-start(s32[2,1,128]{2,1,0:T(1,128)} %seg_ref.3) | copy-start | bytes 3076
  27.5 6.7 %collective-permute-start.6 = (bf16[2,2,16,576]{3,2,0,1:T(8,128)(2,1)S(1)}, bf16[2,2,16,576]{3,2,0,1:T(8,128)(2,1)S(1)}, u32[]{:S(2)}, u32[]{:S(2)}) collective-permute-start(bf16[2,2,16,576]{3,2,0,1:T(8,128)(2,1)S(1)} %fusion.12), channel_id=1, source_target_pairs={{0,2},{1,3},{2,0},{3,1},{4,6},{5,7},{6,4},{7,5},{8,10},{9,11},{10,... | collective-permute-start | bytes 221192 | tf_op jit(solution)/shard_map/ppermute | solution.py:280
  34.3 10.2 %collective-permute-start.7 = (bf16[2,1,16,576]{3,2,1,0:T(8,128)(2,1)S(1)}, bf16[2,1,16,576]{3,2,1,0:T(8,128)(2,1)S(1)}, u32[]{:S(2)}, u32[]{:S(2)}) collective-permute-start(bf16[2,1,16,576]{3,2,1,0:T(8,128)(2,1)S(1)} %fusion.14), channel_id=1, source_target_pairs={{0,4},{1,5},{2,6},{3,7},{4,0},{5,1},{6,2},{7,3},{8,12},{9,13},{10,... | collective-permute-start | bytes 110600 | tf_op jit(solution)/shard_map/ppermute | solution.py:280
  45.1 98.1 %collective-permute-start.8 = (bf16[128,1536]{1,0:T(8,128)(2,1)}, bf16[128,1536]{1,0:T(8,128)(2,1)S(1)}, u32[]{:S(2)}, u32[]{:S(2)}) collective-permute-start(bf16[128,1536]{1,0:T(8,128)(2,1)} %get-tuple-element.45), channel_id=1, source_target_pairs={{1,65},{3,67},{5,69},{7,71},{64,0},{65,129},{66,2},{67,131},{68,4}... | collective-permute-start | bytes 1179656 | tf_op jit(solution)/shard_map/ppermute | solution.py:253
  47.1 96.2 %collective-permute-start.9 = (bf16[128,1536]{1,0:T(8,128)(2,1)}, bf16[128,1536]{1,0:T(8,128)(2,1)S(1)}, u32[]{:S(2)}, u32[]{:S(2)}) collective-permute-start(bf16[128,1536]{1,0:T(8,128)(2,1)} %get-tuple-element.46), channel_id=1, source_target_pairs={{0,64},{2,66},{4,68},{6,70},{64,128},{65,1},{66,130},{67,3},{68,13... | collective-permute-start | bytes 1179656 | tf_op jit(solution)/shard_map/ppermute | solution.py:253
  66.7 10.0 %collective-permute-start = (bf16[2,256,2048]{2,1,0:T(8,128)(2,1)}, bf16[2,256,2048]{2,1,0:T(8,128)(2,1)S(1)}, u32[]{:S(2)}, u32[]{:S(2)}) collective-permute-start(bf16[2,256,2048]{2,1,0:T(8,128)(2,1)} %get-tuple-element.19), channel_id=1, source_target_pairs={{0,8},{8,0},{16,24},{24,16},{32,40},{40,32},{48,56},{56,48},{1,9},... | collective-permute-start | bytes 6291464 | tf_op jit(solution)/shard_map/cond/branch_1_fun/ppermute | solution.py:257
  79.4 15.6 %collective-permute-start.1 = (bf16[2,64,2048]{2,1,0:T(8,128)(2,1)S(1)}, bf16[2,64,2048]{2,1,0:T(8,128)(2,1)S(1)}, u32[]{:S(2)}, u32[]{:S(2)}) collective-permute-start(bf16[2,64,2048]{2,1,0:T(8,128)(2,1)S(1)} %get-tuple-element.21), channel_id=1, source_target_pairs={{0,48},{8,56},{16,0},{24,8},{32,16},{40,24},{48,32},{56,40},{1,49}... | collective-permute-start | bytes 1572872 | tf_op jit(solution)/shard_map/cond/branch_1_fun/ppermute | solution.py:261
  84.1 15.9 %collective-permute-start.2 = (bf16[2,64,2048]{2,1,0:T(8,128)(2,1)S(1)}, bf16[2,64,2048]{2,1,0:T(8,128)(2,1)S(1)}, u32[]{:S(2)}, u32[]{:S(2)}) collective-permute-start(bf16[2,64,2048]{2,1,0:T(8,128)(2,1)S(1)} %get-tuple-element.23), channel_id=1, source_target_pairs={{0,16},{8,24},{16,32},{24,40},{32,48},{40,56},{48,0},{56,8},{1,17}... | collective-permute-start | bytes 1572872 | tf_op jit(solution)/shard_map/cond/branch_1_fun/ppermute | solution.py:260
  101.0 8.5 %collective-permute-start.4 = (bf16[64,2048]{1,0:T(8,128)(2,1)}, bf16[64,2048]{1,0:T(8,128)(2,1)}, u32[]{:S(2)}, u32[]{:S(2)}) collective-permute-start(bf16[64,2048]{1,0:T(8,128)(2,1)} %get-tuple-element.57), channel_id=1, source_target_pairs={{0,48},{8,56},{16,0},{24,8},{32,16},{40,24},{48,32},{56,40},{1,49}... | collective-permute-start | bytes 786440 | tf_op jit(solution)/shard_map/cond/branch_1_fun/ppermute | solution.py:265
  102.9 9.7 %collective-permute-start.3 = (bf16[64,2048]{1,0:T(8,128)(2,1)}, bf16[64,2048]{1,0:T(8,128)(2,1)}, u32[]{:S(2)}, u32[]{:S(2)}) collective-permute-start(bf16[64,2048]{1,0:T(8,128)(2,1)} %get-tuple-element.58), channel_id=1, source_target_pairs={{0,16},{8,24},{16,32},{24,40},{32,48},{40,56},{48,0},{56,8},{1,17}... | collective-permute-start | bytes 786440 | tf_op jit(solution)/shard_map/cond/branch_1_fun/ppermute | solution.py:264
  114.7 71.3 %collective-permute-start.10 = (bf16[64,2048]{1,0:T(8,128)(2,1)}, bf16[64,2048]{1,0:T(8,128)(2,1)S(1)}, u32[]{:S(2)}, u32[]{:S(2)}) collective-permute-start(bf16[64,2048]{1,0:T(8,128)(2,1)} %get-tuple-element.52), channel_id=1, source_target_pairs={{0,960},{64,896},{128,832},{192,768},{256,704},{320,640},{384,576}... | collective-permute-start | bytes 786440 | tf_op jit(solution)/shard_map/ppermute | solution.py:311
  129.3 56.8 %collective-permute-start.12 = (bf16[16,576]{1,0:T(8,128)(2,1)S(1)}, bf16[16,576]{1,0:T(8,128)(2,1)S(1)}, u32[]{:S(2)}, u32[]{:S(2)}) collective-permute-start(bf16[16,576]{1,0:T(8,128)(2,1)S(1)} %get-tuple-element.63), channel_id=1, source_target_pairs={{0,64},{2,66},{4,68},{6,70},{64,128},{65,1},{66,130},{67,3},{68,13... | collective-permute-start | bytes 55304 | tf_op jit(solution)/shard_map/ppermute | solution.py:253
  131.2 54.8 %collective-permute-start.11 = (bf16[16,576]{1,0:T(8,128)(2,1)S(1)}, bf16[16,576]{1,0:T(8,128)(2,1)S(1)}, u32[]{:S(2)}, u32[]{:S(2)}) collective-permute-start(bf16[16,576]{1,0:T(8,128)(2,1)S(1)} %get-tuple-element.64), channel_id=1, source_target_pairs={{1,65},{3,67},{5,69},{7,71},{64,0},{65,129},{66,2},{67,131},{68,4}... | collective-permute-start | bytes 55304 | tf_op jit(solution)/shard_map/ppermute | solution.py:253
  186.0 1.1 copy-start.1

commit v3 on v2

--- a/solution.py
+++ b/solution.py
@@ -25,93 +25,79 @@
     return lax.dot_general(a, b, dims, preferred_element_type=F32)
 
 
-def attention_kernel(side_ref, q_ref, lat_ref, og_ref, seg_ref, w_ref, qg_ref, kvg_ref, rows_ref, allowed_ref, rope_ref, total_ref):
+def attention_kernel(first_ref, q_ref, lat_ref, og_ref, seg_ref, w_ref, qg0_ref, qg1_ref, kvg_ref, rows_ref):
     step = pl.program_id(0)
     tokens = q_ref.shape[2]
-
-    @pl.when(step == 0)
-    def _():
-        across = jnp.broadcast_to(seg_ref[0].astype(F32), (tokens, tokens))
-        rows = lax.broadcasted_iota(jnp.int32, (tokens, tokens), 0)
-        cols = lax.broadcasted_iota(jnp.int32, (tokens, tokens), 1)
-        same = (across == across.T) & (rows >= cols)
-        allowed_ref[...] = jnp.where(same, 1.0, 0.0)
-        rope_ref[...] = jnp.zeros_like(rope_ref)
-        total_ref[...] = jnp.zeros_like(total_ref)
-
-    allowed = allowed_ref[...] > 0.5
-    latents = lat_ref[0, 0]
-    plain, key_rope = latents[:, :LATENT], latents[:, LATENT:]
+    heads = range(w_ref.shape[3] // KVDIM)
+    across = jnp.broadcast_to(seg_ref[0].astype(F32), (tokens, tokens))
+    down = lax.broadcasted_iota(jnp.int32, (tokens, tokens), 0)
+    cols = lax.broadcasted_iota(jnp.int32, (tokens, tokens), 1)
+    allowed = (across == across.T) & (down >= cols)
+    plain, key_rope = lat_ref[0, 0, :LATENT, :].T, lat_ref[0, 0, LATENT:, :].T
     kv = dot(plain, w_ref[0, 0], NN).astype(BF16)
     scale = QDIM ** (-0.5)
-    for h in range(2):
-        query = q_ref[0, 0, :, h * QDIM : (h + 1) * QDIM]
-        out_grad = og_ref[0, 0, :, h * VDIM : (h + 1) * VDIM]
-        key = kv[:, h * KVDIM : h * KVDIM + NOPE]
-        value = kv[:, h * KVDIM + NOPE : (h + 1) * KVDIM]
-        key_all = jnp.concatenate([key, key_rope], 1)
-        scores = jnp.where(allowed, dot(query, key_all, NT) * scale, -1e30)
-        powers = jnp.exp(scores - jnp.max(scores, axis=-1, keepdims=True))
-        probs = powers / jnp.sum(powers, axis=-1, keepdims=True)
-        grad_probs = dot(out_grad, value, NT)
-        delta = jnp.sum(probs * grad_probs, axis=-1, keepdims=True)
-        score_grad = (probs * (grad_probs - delta) * scale).astype(BF16)
-        qg_ref[:, h * QDIM : (h + 1) * QDIM] = dot(score_grad, key_all, NN).astype(BF16)
-        key_grad = dot(score_grad, query, TN)
-        value_grad = dot(probs.astype(BF16), out_grad, TN)
-        kvg_ref[:, h * KVDIM : h * KVDIM + NOPE] = key_grad[:, :NOPE].astype(BF16)
-        kvg_ref[:, h * KVDIM + NOPE : (h + 1) * KVDIM] = value_grad.astype(BF16)
-        rope_ref[...] += key_grad[:, NOPE:]
-    total_ref[...] += dot(kvg_ref[...], w_ref[0, 0], NT)
-
-    @pl.when(step == pl.num_programs(0) - 1)
-    def _():
-        rows_ref[:, :LATENT] = total_ref[...].astype(BF16)
-        rows_ref[:, LATENT:] = rope_ref[...].astype(BF16)
-
-
-def attention(side, queries, latents, out_grad, segment_ids, up_weight):
+    query = [q_ref[0, 0, :, h * QDIM : (h + 1) * QDIM] for h in heads]
+    out_grad = [og_ref[0, 0, :, h * VDIM : (h + 1) * VDIM] for h in heads]
+    key = [jnp.concatenate([kv[:, h * KVDIM : h * KVDIM + NOPE], key_rope], 1) for h in heads]
+    scores = [dot(query[h], key[h], NT) for h in heads]
+    grad_probs = [dot(out_grad[h], kv[:, h * KVDIM + NOPE : (h + 1) * KVDIM], NT) for h in heads]
+    scores = [jnp.where(allowed, x * scale, -1e30) for x in scores]
+    powers = [jnp.exp(x - jnp.max(x, axis=-1, keepdims=True)) for x in scores]
+    probs = [x / jnp.sum(x, axis=-1, keepdims=True) for x in powers]
+    delta = [jnp.sum(probs[h] * grad_probs[h], axis=-1, keepdims=True) for h in heads]
+    score_grad = [(probs[h] * (grad_probs[h] - delta[h]) * scale).astype(BF16) for h in heads]
+    query_grad = [dot(score_grad[h], key[h], NN) for h in heads]
+    value_grad = [dot(probs[h].astype(BF16), out_grad[h], TN) for h in heads]
+    key_grad = [dot(score_grad[h], query[h], TN) for h in heads]
+    for h in heads:
+        kvg_ref[0, :, h * KVDIM : h * KVDIM + NOPE] = key_grad[h][:, :NOPE].astype(BF16)
+        kvg_ref[0, :, h * KVDIM + NOPE : (h + 1) * KVDIM] = value_grad[h].astype(BF16)
+    rows_ref[0, :, :LATENT] = dot(kvg_ref[0], w_ref[0, 0], NT).astype(BF16)
+    rows_ref[0, :, LATENT:] = sum(x[:, NOPE:] for x in key_grad).astype(BF16)
+    for turn, qg_ref in enumerate((qg0_ref, qg1_ref)):
+
+        @pl.when(step == turn)
+        def _():
+            for h in heads:
+                qg_ref[:, h * QDIM : (h + 1) * QDIM] = query_grad[h].astype(BF16)
+
+
+def attention(first, queries, latents, out_grad, segment_ids, up_weight):
     tokens, width = queries.shape[2], up_weight.shape[3]
-    pairs = width // (2 * KVDIM)
+
+    def whole(shape, order):
+        return pl.BlockSpec((1, *shape), lambda i, s: (jnp.where(i == 0, s[0], 1 - s[0]) if order else i,) + (0,) * len(shape))
+
     return pl.pallas_call(
         attention_kernel,
         grid_spec=pltpu.PrefetchScalarGridSpec(
             num_scalar_prefetch=1,
-            grid=(pairs,),
-            in_specs=[
-                pl.BlockSpec((1, 1, tokens, 2 * QDIM), lambda j, s: (s[0], 0, 0, j)),
-                pl.BlockSpec((1, 1, tokens, LATENT + ROPE), lambda j, s: (s[0], 0, 0, 0)),
-                pl.BlockSpec((1, 1, tokens, 2 * VDIM), lambda j, s: (s[0], 0, 0, j)),
-                pl.BlockSpec((1, 1, tokens), lambda j, s: (s[0], 0, 0)),
-                pl.BlockSpec((1, 1, LATENT, 2 * KVDIM), lambda j, s: (s[0], 0, 0, j)),
+            grid=(2,),
+            in_specs=[whole(a.shape[1:], True) for a in (queries, latents, out_grad, segment_ids, up_weight)],
+            out_specs=[
+                pl.BlockSpec(queries.shape[2:], lambda i, s: (0, 0)),
+                pl.BlockSpec(queries.shape[2:], lambda i, s: (0, 0)),
+                whole((tokens, width), False),
+                whole((tokens, LATENT + ROPE), True),
             ],
-            out_specs=[
-                pl.BlockSpec((tokens, 2 * QDIM), lambda j, s: (0, j)),
-                pl.BlockSpec((tokens, 2 * KVDIM), lambda j, s: (0, j)),
-                pl.BlockSpec((tokens, LATENT + ROPE), lambda j, s: (0, 0)),
-            ],
-            scratch_shapes=[
-                pltpu.VMEM((tokens, tokens), F32),
-                pltpu.VMEM((tokens, ROPE), F32),
-                pltpu.VMEM((tokens, LATENT), F32),
-            ],
         ),
         out_shape=[
-            jax.ShapeDtypeStruct((tokens, pairs * 2 * QDIM), BF16),
-            jax.ShapeDtypeStruct((tokens, width), BF16),
-            jax.ShapeDtypeStruct((tokens, LATENT + ROPE), BF16),
+            jax.ShapeDtypeStruct(queries.shape[2:], BF16),
+            jax.ShapeDtypeStruct(queries.shape[2:], BF16),
+            jax.ShapeDtypeStruct((2, tokens, width), BF16),
+            jax.ShapeDtypeStruct((2, tokens, LATENT + ROPE), BF16),
         ],
         compiler_params=pltpu.CompilerParams(vmem_limit_bytes=58 * 1024 * 1024),
         cost_estimate=COST,
-    )(side, queries, latents, out_grad, segment_ids, up_weight)
-
-
-def partial_kernel(who_ref, kvg0_ref, kvg1_ref, lat_ref, keep_ref, send_ref):
+    )(first, queries, latents, out_grad, segment_ids, up_weight)
+
+
+def partial_kernel(who_ref, kvg_ref, lat_ref, keep_ref, send_ref):
     first, core = who_ref[0], who_ref[1]
     shard = keep_ref.shape[1] // 4
-    for i, kvg_ref in enumerate((kvg0_ref, kvg1_ref)):
+    for i in range(2):
         side = first if i == 0 else 1 - first
-        part = dot(lat_ref[side, 0, :, :LATENT], kvg_ref[...], TN)
+        part = dot(lat_ref[side, 0, :LATENT, :], kvg_ref[i], NN)
         for y in range(4):
             low = part[(2 * y) * shard : (2 * y + 1) * shard]
             high = part[(2 * y + 1) * shard : (2 * y + 2) * shard]
@@ -120,7 +106,7 @@
 
 
 def partials(who, kv_grads, latents):
-    tokens, width = kv_grads[0].shape
+    tokens, width = kv_grads.shape[1:]
     cols = 512
     return pl.pallas_call(
         partial_kernel,
@@ -128,8 +114,7 @@
             num_scalar_prefetch=1,
             grid=(width // cols,),
             in_specs=[
-                pl.BlockSpec((tokens, cols), lambda j, s: (0, j)),
-                pl.BlockSpec((tokens, cols), lambda j, s: (0, j)),
+                pl.BlockSpec((2, tokens, cols), lambda j, s: (0, 0, j)),
                 pl.BlockSpec(latents.shape, lambda j, s: (0, 0, 0, 0)),
             ],
             out_specs=[
@@ -143,7 +128,7 @@
         ],
         compiler_params=pltpu.CompilerParams(vmem_limit_bytes=32 * 1024 * 1024),
         cost_estimate=COST,
-    )(who, *kv_grads, latents)
+    )(who, kv_grads, latents)
 
 
 def pair_kernel(y_ref, keep_ref, came_ref, *out_refs):
@@ -291,15 +276,11 @@
     core, y = lax.rem(dp, 2).astype(jnp.int32), lax.div(dp, 2).astype(jnp.int32)
     sections = lax.axis_size("section")
 
-    query_grads, kv_grads, rows = zip(
-        *[
-            attention((first if i == 0 else 1 - first)[None], queries, latents, out_grad, segment_ids, up_weight)
-            for i in range(2)
-        ]
-    )
-    part = sum_over_heads(in_order(first, *rows))
+    across = jnp.swapaxes(latents, 2, 3)
+    *query_grads, kv_grads, rows = attention(first[None], queries, across, out_grad, segment_ids, up_weight)
+    part = sum_over_heads(rows)
     part = in_order(first, part[0], part[1])
-    keep, send = partials(jnp.stack([first, core]), kv_grads, latents)
+    keep, send = partials(jnp.stack([first, core]), kv_grads, across)
     query_grads = held(part, query_grads)
     arrived = [relay(query_grads[i], i) for i in range(2)]
     latent_here = [relay(part[i], i) for i in range(2)]

time: 190 us -> 180 us (0.947)
  Pallas kernels: 26.4 us -> 17.5 us
    pallas_call x2 -> x1, Pallas kernels: 16.3 us -> 7.49 us  [attention(): pl.pallas_call(attention_kernel, grid_spec=pltpu.PrefetchScalarGridSpec(n...]
  transfers between devices with their start and end apart: 13 -> 13, of which waited for: 9 -> 9; matrix products, arithmetic and copies ran while one was open for 2% -> 2% of each run, Pallas kernels for 4% -> 5%
where the time goes in v3:
time: 180 us; the launch traced here: 179 us
  starting transfers between devices  79.9 us (44%)
  waiting for transfers between devices  72.5 us (40%)
  Pallas kernels  17.5 us (10%)
  other arithmetic  6.19 us (3%)
    ppermute x1, waiting for transfers between devices, body(): lax.ppermute(reverse, 'section', [(i, sections - 1 - i) for i in range(se...  41.4 us
    ppermute x4, starting transfers between devices, relay(): return lax.ppermute(block, ('section', 'head'), route)  30.2 us
    ppermute x3, starting transfers between devices, sum_over_heads(): lax.ppermute(sent, 'head', [(i, i ^ 1 << bit) for i in range(8)])  17.3 us
    ppermute x1, starting transfers between devices, body(): lax.ppermute(reverse, 'section', [(i, sections - 1 - i) for i in range(se...  14.6 us
    ppermute x1, waiting for transfers between devices, sum_over_replicas(): from_above = lax.ppermute(down, 'dp', below).astype(F32)  8.99 us
    pallas_call x1, Pallas kernels, attention(): pl.pallas_call(attention_kernel, grid_spec=pltpu.PrefetchScalarGridSpec(n...  7.49 us
    ppermute x3, waiting for transfers between devices, sum_over_heads(): lax.ppermute(sent, 'head', [(i, i ^ 1 << bit) for i in range(8)])  6.95 us
    ppermute x1, starting transfers between devices, sum_over_replicas(): came = lax.ppermute(send, 'dp', [(i, i ^ 1) for i in range(8)])  6.03 us
  transfers between devices with their start and end apart: 13, of which 9 were waited for; matrix products, arithmetic and copies ran while one was open for 2% of the time, Pallas kernels for 5%

profile of v3, /device:TPU:257, one launch (start us, length us, event | category | flops | bytes accessed | tf_op | source)
XLA Modules:
  0.0 179.3 jit_solution(10990308087610952528)
XLA Ops:
  0.6 7.5 %shard_map.76 = (bf16[128,1536]{1,0:T(8,128)(2,1)}, bf16[128,1536]{1,0:T(8,128)(2,1)}, bf16[2,128,2048]{2,1,0:T(8,128)(2,1)}, bf16[2,128,576]{2,1,0:T(8,128)(2,1)}) custom-call(s32[1]{0:T(128)} %bitcast.5.first_ref, bf16[2,1,128,1536]{3,2,1,0:T(8,128)(2,1)} %q_ref.1, bf16[2,1,576,128]{3,2,1,0:T(8,128)(2,1)} %bitcast.68, bf16[2,1,128,1024]{3,2,1,0:T(8,128)(2,1)} %og_ref.1, ...), custom_call_target="tpu_custom_call" | custom-call | flops 1000 | bytes 1000 | tf_op jit(solution)/shard_map/pallas_call | solution.py:71
  9.3 3.5 %collective-permute-start.5 = (bf16[2,4,16,576]{3,2,1,0:T(8,128)(2,1)S(1)}, bf16[2,4,16,576]{3,2,1,0:T(8,128)(2,1)S(1)}, u32[]{:S(2)}, u32[]{:S(2)}) collective-permute-start(bf16[2,4,16,576]{3,2,1,0:T(8,128)(2,1)S(1)} %select_bitcast_fusion), channel_id=1, source_target_pairs={{0,1},{1,0},{2,3},{3,2},{4,5},{5,4},{6,7},{7,6},{8,9},{9,8},{10,11... | collective-permute-start | bytes 442376 | tf_op jit(solution)/shard_map/ppermute | solution.py:265
  12.8 3.8 %collective-permute-done.5 = bf16[2,4,16,576]{3,2,1,0:T(8,128)(2,1)S(1)} collective-permute-done((bf16[2,4,16,576]{3,2,1,0:T(8,128)(2,1)S(1)}, bf16[2,4,16,576]{3,2,1,0:T(8,128)(2,1)S(1)}, u32[]{:S(2)}, u32[]{:S(2)}) %collective-permute-start.5) | collective-permute-done | bytes 147488 | tf_op jit(solution)/shard_map/ppermute | solution.py:265
  17.7 4.9 %collective-permute-start.6 = (bf16[2,2,16,576]{3,2,0,1:T(8,128)(2,1)S(1)}, bf16[2,2,16,576]{3,2,0,1:T(8,128)(2,1)S(1)}, u32[]{:S(2)}, u32[]{:S(2)}) collective-permute-start(bf16[2,2,16,576]{3,2,0,1:T(8,128)(2,1)S(1)} %fusion.9), channel_id=1, source_target_pairs={{0,2},{1,3},{2,0},{3,1},{4,6},{5,7},{6,4},{7,5},{8,10},{9,11},{10,... | collective-permute-start | bytes 221192 | tf_op jit(solution)/shard_map/ppermute | solution.py:265
  24.5 8.8 %collective-permute-start.7 = (bf16[2,1,16,576]{3,2,1,0:T(8,128)(2,1)S(1)}, bf16[2,1,16,576]{3,2,1,0:T(8,128)(2,1)S(1)}, u32[]{:S(2)}, u32[]{:S(2)}) collective-permute-start(bf16[2,1,16,576]{3,2,1,0:T(8,128)(2,1)S(1)} %fusion.11), channel_id=1, source_target_pairs={{0,4},{1,5},{2,6},{3,7},{4,0},{5,1},{6,2},{7,3},{8,12},{9,13},{10,... | collective-permute-start | bytes 110600 | tf_op jit(solution)/shard_map/ppermute | solution.py:265
  37.3 14.3 %collective-permute-start.9 = (bf16[128,1536]{1,0:T(8,128)(2,1)}, bf16[128,1536]{1,0:T(8,128)(2,1)S(1)}, u32[]{:S(2)}, u32[]{:S(2)}) collective-permute-start(bf16[128,1536]{1,0:T(8,128)(2,1)} %get-tuple-element.43), channel_id=1, source_target_pairs={{0,64},{2,66},{4,68},{6,70},{64,128},{65,1},{66,130},{67,3},{68,13... | collective-permute-start | bytes 1179656 | tf_op jit(solution)/shard_map/ppermute | solution.py:238
  51.7 3.9 %shard_map.79 = (bf16[2,256,2048]{2,1,0:T(8,128)(2,1)}, bf16[2,256,2048]{2,1,0:T(8,128)(2,1)}) custom-call(s32[2]{0:T(128)S(1)} %pad_add_fusion.who_ref, bf16[2,128,2048]{2,1,0:T(8,128)(2,1)S(1)} %copy-done.2, bf16[2,1,576,128]{3,2,1,0:T(8,128)(2,1)S(1)} %bitcast.69), custom_call_target="tpu_custom_call" | custom-call | flops 1000 | bytes 1000 | tf_op jit(solution)/shard_map/pallas_call | solution.py:111
  56.8 48.0 %conditional.1 = (f32[64,2048]{1,0:T(8,128)}, bf16[64,2048]{1,0:T(8,128)(2,1)}) conditional(s32[]{:T(128)} %bitcast.19, () %tuple.16, (s32[]{:T(128)}, s32[]{:T(128)}, pred[]{:T(512)}, bf16[2,256,2048]{2,1,0:T(8,128)(2,1)}, bf16[2,256,2048]{2,1,0:T(8,128)(2,1)}) %tuple.17), branch_computations={%region_0.1_spmd, %region_1.2_spmd} | conditional | flops 2753516 | bytes 22807788 | solution.py:290
  56.8 6.0 %collective-permute-start = (bf16[2,256,2048]{2,1,0:T(8,128)(2,1)}, bf16[2,256,2048]{2,1,0:T(8,128)(2,1)S(1)}, u32[]{:S(2)}, u32[]{:S(2)}) collective-permute-start(bf16[2,256,2048]{2,1,0:T(8,128)(2,1)} %get-tuple-element.19), channel_id=1, source_target_pairs={{0,8},{8,0},{16,24},{24,16},{32,40},{40,32},{48,56},{56,48},{1,9},... | collective-permute-start | bytes 6291464 | tf_op jit(solution)/shard_map/cond/branch_1_fun/ppermute | solution.py:242
  62.9 4.0 %collective-permute-done.came_ref = bf16[2,256,2048]{2,1,0:T(8,128)(2,1)S(1)} collective-permute-done((bf16[2,256,2048]{2,1,0:T(8,128)(2,1)}, bf16[2,256,2048]{2,1,0:T(8,128)(2,1)S(1)}, u32[]{:S(2)}, u32[]{:S(2)}) %collective-permute-start) | collective-permute-done | bytes 2097184 | tf_op jit(solution)/shard_map/cond/branch_1_fun/ppermute | solution.py:242
  66.8 2.7 %branch_1_fun.1 = (bf16[2,64,2048]{2,1,0:T(8,128)(2,1)S(1)}, bf16[2,64,2048]{2,1,0:T(8,128)(2,1)S(1)}, bf16[2,64,2048]{2,1,0:T(8,128)(2,1)S(1)}, bf16[2,64,2048]{2,1,0:T(8,128)(2,1)S(1)}) custom-call(s32[1]{0:T(128)} %bitcast.y_ref, bf16[2,256,2048]{2,1,0:T(8,128)(2,1)} %get-tuple-element.18.keep_ref, bf16[2,256,2048]{2,1,0:T(8,128)(2,1)S(1)} %collective-permute-done.came_ref), custom_call_target="tpu_custom_call" | custom-call | flops 1000 | bytes 1000 | tf_op jit(solution)/shard_map/cond/branch_1_fun/pallas_call | solution.py:146
  69.5 4.6 %collective-permute-start.1 = (bf16[2,64,2048]{2,1,0:T(8,128)(2,1)S(1)}, bf16[2,64,2048]{2,1,0:T(8,128)(2,1)S(1)}, u32[]{:S(2)}, u32[]{:S(2)}) collective-permute-start(bf16[2,64,2048]{2,1,0:T(8,128)(2,1)S(1)} %get-tuple-element.21), channel_id=1, source_target_pairs={{0,48},{8,56},{16,0},{24,8},{32,16},{40,24},{48,32},{56,40},{1,49}... | collective-permute-start | bytes 1572872 | tf_op jit(solution)/shard_map/cond/branch_1_fun/ppermute | solution.py:246
  74.2 1.9 %collective-permute-start.2 = (bf16[2,64,2048]{2,1,0:T(8,128)(2,1)S(1)}, bf16[2,64,2048]{2,1,0:T(8,128)(2,1)S(1)}, u32[]{:S(2)}, u32[]{:S(2)}) collective-permute-start(bf16[2,64,2048]{2,1,0:T(8,128)(2,1)S(1)} %get-tuple-element.23), channel_id=1, source_target_pairs={{0,16},{8,24},{16,32},{24,40},{32,48},{40,56},{48,0},{56,8},{1,17}... | collective-permute-start | bytes 1572872 | tf_op jit(solution)/shard_map/cond/branch_1_fun/ppermute | solution.py:245
  76.1 9.0 %collective-permute-done.1 = bf16[2,64,2048]{2,1,0:T(8,128)(2,1)S(1)} collective-permute-done((bf16[2,64,2048]{2,1,0:T(8,128)(2,1)S(1)}, bf16[2,64,2048]{2,1,0:T(8,128)(2,1)S(1)}, u32[]{:S(2)}, u32[]{:S(2)}) %collective-permute-start.1) | collective-permute-done | bytes 524320 | tf_op jit(solution)/shard_map/cond/branch_1_fun/ppermute | solution.py:246
  85.2 4.9 %collective-permute-done.2 = bf16[2,64,2048]{2,1,0:T(8,128)(2,1)S(1)} collective-permute-done((bf16[2,64,2048]{2,1,0:T(8,128)(2,1)S(1)}, bf16[2,64,2048]{2,1,0:T(8,128)(2,1)S(1)}, u32[]{:S(2)}, u32[]{:S(2)}) %collective-permute-start.2) | collective-permute-done | bytes 524320 | tf_op jit(solution)/shard_map/cond/branch_1_fun/ppermute | solution.py:245
  91.1 1.9 %collective-permute-start.4 = (bf16[64,2048]{1,0:T(8,128)(2,1)}, bf16[64,2048]{1,0:T(8,128)(2,1)}, u32[]{:S(2)}, u32[]{:S(2)}) collective-permute-start(bf16[64,2048]{1,0:T(8,128)(2,1)} %get-tuple-element.53), channel_id=1, source_target_pairs={{0,48},{8,56},{16,0},{24,8},{32,16},{40,24},{48,32},{56,40},{1,49}... | collective-permute-start | bytes 786440 | tf_op jit(solution)/shard_map/cond/branch_1_fun/ppermute | solution.py:250
  93.0 3.4 %collective-permute-start.3 = (bf16[64,2048]{1,0:T(8,128)(2,1)}, bf16[64,2048]{1,0:T(8,128)(2,1)}, u32[]{:S(2)}, u32[]{:S(2)}) collective-permute-start(bf16[64,2048]{1,0:T(8,128)(2,1)} %get-tuple-element.54), channel_id=1, source_target_pairs={{0,16},{8,24},{16,32},{24,40},{32,48},{40,56},{48,0},{56,8},{1,17}... | collective-permute-start | bytes 786440 | tf_op jit(solution)/shard_map/cond/branch_1_fun/ppermute | solution.py:249
  96.4 3.2 %collective-permute-done.4 = bf16[64,2048]{1,0:T(8,128)(2,1)} collective-permute-done((bf16[64,2048]{1,0:T(8,128)(2,1)}, bf16[64,2048]{1,0:T(8,128)(2,1)}, u32[]{:S(2)}, u32[]{:S(2)}) %collective-permute-start.4) | collective-permute-done | bytes 262176 | tf_op jit(solution)/shard_map/cond/branch_1_fun/ppermute | solution.py:250
  99.6 3.1 %collective-permute-done.3 = bf16[64,2048]{1,0:T(8,128)(2,1)} collective-permute-done((bf16[64,2048]{1,0:T(8,128)(2,1)}, bf16[64,2048]{1,0:T(8,128)(2,1)}, u32[]{:S(2)}, u32[]{:S(2)}) %collective-permute-start.3) | collective-permute-done | bytes 262176 | tf_op jit(solution)/shard_map/cond/branch_1_fun/ppermute | solution.py:249
  102.7 2.1 %select_convert_fusion = (bf16[64,2048]{1,0:T(8,128)(2,1)}, f32[64,2048]{1,0:T(8,128)}) fusion(pred[]{:T(512)S(6)} %eq.0, bf16[64,2048]{1,0:T(8,128)(2,1)} %collective-permute-done.3, f32[2,64,2048]{2,1,0:T(8,128)S(1)} %convert_element_type.64, bf16[2,64,2048]{2,1,0:T(8,128)(2,1)S(1)} %get-tuple-element.20, bf16[64,2048]{1,0:T(8,128)(2,1)} %collective-permute-done.4, ...), kind=kLoop, calls=%fused_computation.10 | loop fusion | flops 1441792 | bytes 2883585 | tf_op jit(solution)/shard_map/cond/branch_1_fun/convert_element_type | solution.py:253
  104.8 14.6 %collective-permute-start.10 = (bf16[64,2048]{1,0:T(8,128)(2,1)}, bf16[64,2048]{1,0:T(8,128)(2,1)S(1)}, u32[]{:S(2)}, u32[]{:S(2)}) collective-permute-start(bf16[64,2048]{1,0:T(8,128)(2,1)} %get-tuple-element.48), channel_id=1, source_target_pairs={{0,960},{64,896},{128,832},{192,768},{256,704},{320,640},{384,576}... | collective-permute-start | bytes 786440 | tf_op jit(solution)/shard_map/ppermute | solution.py:292
  119.4 1.9 %collective-permute-start.12 = (bf16[16,576]{1,0:T(8,128)(2,1)S(1)}, bf16[16,576]{1,0:T(8,128)(2,1)S(1)}, u32[]{:S(2)}, u32[]{:S(2)}) collective-permute-start(bf16[16,576]{1,0:T(8,128)(2,1)S(1)} %get-tuple-element.57), channel_id=1, source_target_pairs={{0,64},{2,66},{4,68},{6,70},{64,128},{65,1},{66,130},{67,3},{68,13... | collective-permute-start | bytes 55304 | tf_op jit(solution)/shard_map/ppermute | solution.py:238
  121.3 12.1 %collective-permute-start.11 = (bf16[16,576]{1,0:T(8,128)(2,1)S(1)}, bf16[16,576]{1,0:T(8,128)(2,1)S(1)}, u32[]{:S(2)}, u32[]{:S(2)}) collective-permute-start(bf16[16,576]{1,0:T(8,128)(2,1)S(1)} %get-tuple-element.58), channel_id=1, source_target_pairs={{1,65},{3,67},{5,69},{7,71},{64,0},{65,129},{66,2},{67,131},{68,4}... | collective-permute-start | bytes 55304 | tf_op jit(solution)/shard_map/ppermute | solution.py:238
  135.0 41.4 %collective-permute-done.10.mirrored_ref = bf16[64,2048]{1,0:T(8,128)(2,1)S(1)} collective-permute-done((bf16[64,2048]{1,0:T(8,128)(2,1)}, bf16[64,2048]{1,0:T(8,128)(2,1)S(1)}, u32[]{:S(2)}, u32[]{:S(2)}) %collective-permute-start.10) | collective-permute-done | bytes 262176 | tf_op jit(solution)/shard_map/ppermute | solution.py:292
  (32 shorter events, 14.2 us)
Async XLA Ops:
  8.1 43.6 %copy-start.1 = (bf16[2,1,128,576]{2,3,1,0:T(8,128)(2,1)S(1)}, bf16[2,1,128,576]{2,3,1,0:T(8,128)(2,1)}, u32[]{:S(2)}) copy-start(bf16[2,1,128,576]{2,3,1,0:T(8,128)(2,1)} %param.8) | copy-start | bytes 884740
  8.1 43.6 %copy-start.2 = (bf16[2,128,2048]{2,1,0:T(8,128)(2,1)S(1)}, bf16[2,128,2048]{2,1,0:T(8,128)(2,1)}, u32[]{:S(2)}) copy-start(bf16[2,128,2048]{2,1,0:T(8,128)(2,1)} %get-tuple-element.44.kvg_ref) | copy-start | bytes 3145732
  9.3 7.3 %collective-permute-start.5 = (bf16[2,4,16,576]{3,2,1,0:T(8,128)(2,1)S(1)}, bf16[2,4,16,576]{3,2,1,0:T(8,128)(2,1)S(1)}, u32[]{:S(2)}, u32[]{:S(2)}) collective-permute-start(bf16[2,4,16,576]{3,2,1,0:T(8,128)(2,1)S(1)} %select_bitcast_fusion), channel_id=1, source_target_pairs={{0,1},{1,0},{2,3},{3,2},{4,5},{5,4},{6,7},{7,6},{8,9},{9,8},{10,11... | collective-permute-start | bytes 442376 | tf_op jit(solution)/shard_map/ppermute | solution.py:265
  17.7 38.0 %copy-start.3 = (s32[2,1,128]{2,1,0:T(1,128)S(1)}, s32[2,1,128]{2,1,0:T(1,128)}, u32[]{:S(2)}) copy-start(s32[2,1,128]{2,1,0:T(1,128)} %seg_ref.1) | copy-start | bytes 3076
  17.7 6.7 %collective-permute-start.6 = (bf16[2,2,16,576]{3,2,0,1:T(8,128)(2,1)S(1)}, bf16[2,2,16,576]{3,2,0,1:T(8,128)(2,1)S(1)}, u32[]{:S(2)}, u32[]{:S(2)}) collective-permute-start(bf16[2,2,16,576]{3,2,0,1:T(8,128)(2,1)S(1)} %fusion.9), channel_id=1, source_target_pairs={{0,2},{1,3},{2,0},{3,1},{4,6},{5,7},{6,4},{7,5},{8,10},{9,11},{10,... | collective-permute-start | bytes 221192 | tf_op jit(solution)/shard_map/ppermute | solution.py:265
  24.5 10.2 %collective-permute-start.7 = (bf16[2,1,16,576]{3,2,1,0:T(8,128)(2,1)S(1)}, bf16[2,1,16,576]{3,2,1,0:T(8,128)(2,1)S(1)}, u32[]{:S(2)}, u32[]{:S(2)}) collective-permute-start(bf16[2,1,16,576]{3,2,1,0:T(8,128)(2,1)S(1)} %fusion.11), channel_id=1, source_target_pairs={{0,4},{1,5},{2,6},{3,7},{4,0},{5,1},{6,2},{7,3},{8,12},{9,13},{10,... | collective-permute-start | bytes 110600 | tf_op jit(solution)/shard_map/ppermute | solution.py:265
  35.4 98.0 %collective-permute-start.8 = (bf16[128,1536]{1,0:T(8,128)(2,1)}, bf16[128,1536]{1,0:T(8,128)(2,1)S(1)}, u32[]{:S(2)}, u32[]{:S(2)}) collective-permute-start(bf16[128,1536]{1,0:T(8,128)(2,1)} %get-tuple-element.42), channel_id=1, source_target_pairs={{1,65},{3,67},{5,69},{7,71},{64,0},{65,129},{66,2},{67,131},{68,4}... | collective-permute-start | bytes 1179656 | tf_op jit(solution)/shard_map/ppermute | solution.py:238
  37.3 96.1 %collective-permute-start.9 = (bf16[128,1536]{1,0:T(8,128)(2,1)}, bf16[128,1536]{1,0:T(8,128)(2,1)S(1)}, u32[]{:S(2)}, u32[]{:S(2)}) collective-permute-start(bf16[128,1536]{1,0:T(8,128)(2,1)} %get-tuple-element.43), channel_id=1, source_target_pairs={{0,64},{2,66},{4,68},{6,70},{64,128},{65,1},{66,130},{67,3},{68,13... | collective-permute-start | bytes 1179656 | tf_op jit(solution)/shard_map/ppermute | solution.py:238
  56.8 10.0 %collective-permute-start = (bf16[2,256,2048]{2,1,0:T(8,128)(2,1)}, bf16[2,256,2048]{2,1,0:T(8,128)(2,1)S(1)}, u32[]{:S(2)}, u32[]{:S(2)}) collective-permute-start(bf16[2,256,2048]{2,1,0:T(8,128)(2,1)} %get-tuple-element.19), channel_id=1, source_target_pairs={{0,8},{8,0},{16,24},{24,16},{32,40},{40,32},{48,56},{56,48},{1,9},... | collective-permute-start | bytes 6291464 | tf_op jit(solution)/shard_map/cond/branch_1_fun/ppermute | solution.py:242
  69.5 15.6 %collective-permute-start.1 = (bf16[2,64,2048]{2,1,0:T(8,128)(2,1)S(1)}, bf16[2,64,2048]{2,1,0:T(8,128)(2,1)S(1)}, u32[]{:S(2)}, u32[]{:S(2)}) collective-permute-start(bf16[2,64,2048]{2,1,0:T(8,128)(2,1)S(1)} %get-tuple-element.21), channel_id=1, source_target_pairs={{0,48},{8,56},{16,0},{24,8},{32,16},{40,24},{48,32},{56,40},{1,49}... | collective-permute-start | bytes 1572872 | tf_op jit(solution)/shard_map/cond/branch_1_fun/ppermute | solution.py:246
  74.2 15.9 %collective-permute-start.2 = (bf16[2,64,2048]{2,1,0:T(8,128)(2,1)S(1)}, bf16[2,64,2048]{2,1,0:T(8,128)(2,1)S(1)}, u32[]{:S(2)}, u32[]{:S(2)}) collective-permute-start(bf16[2,64,2048]{2,1,0:T(8,128)(2,1)S(1)} %get-tuple-element.23), channel_id=1, source_target_pairs={{0,16},{8,24},{16,32},{24,40},{32,48},{40,56},{48,0},{56,8},{1,17}... | collective-permute-start | bytes 1572872 | tf_op jit(solution)/shard_map/cond/branch_1_fun/ppermute | solution.py:245
  91.1 8.5 %collective-permute-start.4 = (bf16[64,2048]{1,0:T(8,128)(2,1)}, bf16[64,2048]{1,0:T(8,128)(2,1)}, u32[]{:S(2)}, u32[]{:S(2)}) collective-permute-start(bf16[64,2048]{1,0:T(8,128)(2,1)} %get-tuple-element.53), channel_id=1, source_target_pairs={{0,48},{8,56},{16,0},{24,8},{32,16},{40,24},{48,32},{56,40},{1,49}... | collective-permute-start | bytes 786440 | tf_op jit(solution)/shard_map/cond/branch_1_fun/ppermute | solution.py:250
  93.0 9.7 %collective-permute-start.3 = (bf16[64,2048]{1,0:T(8,128)(2,1)}, bf16[64,2048]{1,0:T(8,128)(2,1)}, u32[]{:S(2)}, u32[]{:S(2)}) collective-permute-start(bf16[64,2048]{1,0:T(8,128)(2,1)} %get-tuple-element.54), channel_id=1, source_target_pairs={{0,16},{8,24},{16,32},{24,40},{32,48},{40,56},{48,0},{56,8},{1,17}... | collective-permute-start | bytes 786440 | tf_op jit(solution)/shard_map/cond/branch_1_fun/ppermute | solution.py:249
  104.8 71.5 %collective-permute-start.10 = (bf16[64,2048]{1,0:T(8,128)(2,1)}, bf16[64,2048]{1,0:T(8,128)(2,1)S(1)}, u32[]{:S(2)}, u32[]{:S(2)}) collective-permute-start(bf16[64,2048]{1,0:T(8,128)(2,1)} %get-tuple-element.48), channel_id=1, source_target_pairs={{0,960},{64,896},{128,832},{192,768},{256,704},{320,640},{384,576}... | collective-permute-start | bytes 786440 | tf_op jit(solution)/shard_map/ppermute | solution.py:292
  119.4 57.0 %collective-permute-start.12 = (bf16[16,576]{1,0:T(8,128)(2,1)S(1)}, bf16[16,576]{1,0:T(8,128)(2,1)S(1)}, u32[]{:S(2)}, u32[]{:S(2)}) collective-permute-start(bf16[16,576]{1,0:T(8,128)(2,1)S(1)} %get-tuple-element.57), channel_id=1, source_target_pairs={{0,64},{2,66},{4,68},{6,70},{64,128},{65,1},{66,130},{67,3},{68,13... | collective-permute-start | bytes 55304 | tf_op jit(solution)/shard_map/ppermute | solution.py:238
  121.3 55.0 %collective-permute-start.11 = (bf16[16,576]{1,0:T(8,128)(2,1)S(1)}, bf16[16,576]{1,0:T(8,128)(2,1)S(1)}, u32[]{:S(2)}, u32[]{:S(2)}) collective-permute-start(bf16[16,576]{1,0:T(8,128)(2,1)S(1)} %get-tuple-element.58), channel_id=1, source_target_pairs={{1,65},{3,67},{5,69},{7,71},{64,0},{65,129},{66,2},{67,131},{68,4}... | collective-permute-start | bytes 55304 | tf_op jit(solution)/shard_map/ppermute | solution.py:238
  176.4 1.1 copy-start
